TPU v7x, 32 devices: a whole 2x2x4 slice. The times are simulated.
32 devices in a mesh: ctx: 8 (over z, x), dp: 4 (over y, core).
Axes of the slice: x: 2, y: 2, z: 4, core: 2. Of those that a mesh axis runs over, the one named last changes fastest.
Arguments:
- queries: bfloat16 [4, 1024, 512], P('dp', 'ctx'), may hold values from -6 to 6
- keys: bfloat16 [4, 1024, 512], P('dp', 'ctx'), may hold values from -6 to 6
- values: bfloat16 [4, 1024, 512], P('dp', 'ctx'), may hold values from -6 to 6
- global_keys: bfloat16 [128, 512], replicated, may hold values from -6 to 6
- global_values: bfloat16 [128, 512], replicated, may hold values from -6 to 6
- upstream: bfloat16 [4, 1024, 512], P('dp', 'ctx'), may hold values from -6 to 6
- partner_shard: int32 [16, 3], replicated, may hold values from 0 to 7, as said below
- partner_block: int32 [16, 3], replicated, may hold values from 0 to 1
Outputs:
- attention: bfloat16 [4, 1024, 512], P('dp', 'ctx')
- grad_queries: bfloat16 [4, 1024, 512], P('dp', 'ctx')
- grad_keys: bfloat16 [4, 1024, 512], P('dp', 'ctx')
- grad_values: bfloat16 [4, 1024, 512], P('dp', 'ctx')
- grad_global_keys: float32 [128, 512], replicated
- grad_global_values: float32 [128, 512], replicated
Inputs may be any that keep to these rules, and one draw needn't show every extreme that they name: `partner_shard`: row i describes query block i of every sequence, which lies on shard i // 2. Each entry differs from i // 2 in exactly one bit of the shard index. For every shard and every bit, at most 2 of the shard's 2 * 3 entries use that bit, and on every shard some bit is used by exactly 2 of them.
All inputs are finite; a program needn't handle non-finite values.
Results may differ from a plain program's by a relative error of at most 0.0076.
Values may be sent and summed in bfloat16 or wider, within the bound.
A program may use at most 64 MiB of HBM per device.

v0:
```python
import math

import jax
import jax.numpy as jnp
from jax import lax
from jax.sharding import PartitionSpec as P

HEAD_DIM = 64
BLOCK = 64
R = 3


masked_score = -1e30


def partner(value, axis, distance):
    mask = 2**distance
    pairs = [(source, source ^ mask) for source in range(lax.axis_size(axis))]
    return lax.ppermute(value, axis, pairs)


def extended(array, sides, width):
    for axis, dim in sides:
        peers, length = (lax.axis_size(axis), array.shape[dim])
        up = [(i, (i + 1) % peers) for i in range(peers - 1)]
        down = [(j, i) for i, j in up]
        last = lax.slice_in_dim(array, length - width, length, axis=dim)
        leading = lax.slice_in_dim(array, 0, width, axis=dim)
        before = lax.ppermute(last, axis, up)
        after = lax.ppermute(leading, axis, down)
        array = jnp.concatenate([before, array, after], axis=dim)
    return array


def local_valid(block_ids, total_blocks):
    block_count = block_ids.shape[0]
    left_open = jnp.broadcast_to((block_ids > 0)[:, None], (block_count, BLOCK))
    right_open = jnp.broadcast_to((block_ids < total_blocks - 1)[:, None], (block_count, BLOCK))
    center = jnp.ones((block_count, BLOCK), jnp.bool_)
    remote = jnp.ones((block_count, R * BLOCK), jnp.bool_)
    return jnp.concatenate([left_open, center, right_open, remote], axis=1)


def head_view(rows, head_count):
    return rows.reshape(rows.shape[0], rows.shape[1], head_count, HEAD_DIM)


def slot_table(wanted, capacity):
    slot_rank = jnp.cumsum(wanted) - wanted
    slot_ids = jnp.arange(capacity, dtype=jnp.int32)
    return ((wanted[:, None] == 1) & (slot_rank[:, None] == slot_ids[None, :])).astype(jnp.float32)


def entry_terms(grad_scores, probs_low, query_heads, grad_heads, first, last):
    block_count = query_heads.shape[0]
    full_width = query_heads.shape[2] * HEAD_DIM
    key_terms = jnp.einsum(
        "nhqk,nqhd->nkhd", grad_scores, query_heads, preferred_element_type=jnp.float32
    ).reshape(block_count, last - first, full_width)
    value_terms = jnp.einsum(
        "nhqk,nqhd->nkhd", probs_low, grad_heads, preferred_element_type=jnp.float32
    ).reshape(block_count, last - first, full_width)
    return jnp.concatenate([key_terms, value_terms], axis=2)


def body(queries, keys, values, global_keys, global_values, upstream, partner_shard, partner_block):
    shard_count = lax.axis_size("ctx")
    bit_count = shard_count.bit_length() - 1
    shard_index = lax.axis_index("ctx")
    rows_dev = queries.shape[1]
    full_width = queries.shape[2]
    pair_width = 2 * full_width
    head_count = full_width // HEAD_DIM
    blocks_dev = rows_dev // BLOCK
    requests = blocks_dev * R
    capacity = max(2, (requests + bit_count - 1) // bit_count)
    total_blocks = blocks_dev * shard_count
    global_count = global_keys.shape[0]
    first_block = shard_index * blocks_dev
    block_range = jnp.arange(blocks_dev, dtype=jnp.int32)
    scaling = 1.0 / math.sqrt(HEAD_DIM)
    own_shards = lax.dynamic_slice_in_dim(partner_shard, first_block, blocks_dev, 0).reshape(
        requests
    )
    receive_tables = []
    send_tables = []
    for bit_index in range(bit_count):
        stride = 1 << bit_index
        peer_shard = shard_index + stride * (1 - 2 * (shard_index // stride % 2))
        receive_tables.append(slot_table((own_shards == peer_shard).astype(jnp.int32), capacity))
        peer_shards = lax.dynamic_slice_in_dim(
            partner_shard, peer_shard * blocks_dev, blocks_dev, 0
        ).reshape(requests)
        peer_blocks = lax.dynamic_slice_in_dim(
            partner_block, peer_shard * blocks_dev, blocks_dev, 0
        ).reshape(requests)
        chosen = slot_table((peer_shards == shard_index).astype(jnp.int32), capacity)
        block_hot = (peer_blocks[:, None] == block_range[None, :]).astype(jnp.float32)
        send_tables.append(
            jnp.dot(chosen.T, block_hot, precision=lax.Precision.HIGHEST).astype(jnp.bfloat16)
        )
    receive_hot = jnp.concatenate(receive_tables, axis=1).astype(jnp.bfloat16)
    pair_rows = jnp.concatenate([keys[0], values[0]], axis=1)
    pair_blocks = pair_rows.reshape(blocks_dev, BLOCK * pair_width)
    arrived = []
    for bit_index in range(bit_count):
        outgoing = jnp.dot(
            send_tables[bit_index], pair_blocks, preferred_element_type=jnp.float32
        ).astype(jnp.bfloat16)
        arrived.append(partner(outgoing, "ctx", bit_index))
    gathered = jnp.concatenate(arrived, axis=0)
    partner_rows = jnp.dot(receive_hot, gathered, preferred_element_type=jnp.float32).astype(
        jnp.bfloat16
    )
    partner_rows = partner_rows.reshape(blocks_dev, R * BLOCK, pair_width)
    padded = extended(pair_rows, (("ctx", 0),), BLOCK)
    window_view = padded.reshape(blocks_dev + 2, BLOCK, pair_width)
    local_rows = jnp.concatenate(
        [
            window_view[0:blocks_dev],
            window_view[1 : blocks_dev + 1],
            window_view[2 : blocks_dev + 2],
            partner_rows,
        ],
        axis=1,
    )
    valid_keys = local_valid(first_block + block_range, total_blocks)
    query_heads = queries[0].reshape(blocks_dev, BLOCK, head_count, HEAD_DIM)
    grad_heads = upstream[0].reshape(blocks_dev, BLOCK, head_count, HEAD_DIM)
    local_keys = head_view(local_rows[:, :, :full_width], head_count)
    local_values = head_view(local_rows[:, :, full_width:], head_count)
    shared_keys = global_keys.reshape(global_count, head_count, HEAD_DIM)
    shared_values = global_values.reshape(global_count, head_count, HEAD_DIM)
    local_scores = (
        jnp.einsum("nqhd,nkhd->nhqk", query_heads, local_keys, preferred_element_type=jnp.float32)
        * scaling
    )
    local_scores = jnp.where(valid_keys[:, None, None, :], local_scores, masked_score)
    shared_scores = (
        jnp.einsum("nqhd,khd->nhqk", query_heads, shared_keys, preferred_element_type=jnp.float32)
        * scaling
    )
    row_max = jnp.maximum(
        jnp.max(local_scores, axis=3, keepdims=True), jnp.max(shared_scores, axis=3, keepdims=True)
    )
    total = jnp.sum(jnp.exp(local_scores - row_max), axis=3, keepdims=True) + jnp.sum(
        jnp.exp(shared_scores - row_max), axis=3, keepdims=True
    )
    local_probs = jnp.exp(local_scores - row_max) / total
    shared_probs = jnp.exp(shared_scores - row_max) / total
    local_low = local_probs.astype(jnp.bfloat16)
    shared_low = shared_probs.astype(jnp.bfloat16)
    attention = jnp.einsum(
        "nhqk,nkhd->nqhd", local_low, local_values, preferred_element_type=jnp.float32
    ) + jnp.einsum("nhqk,khd->nqhd", shared_low, shared_values, preferred_element_type=jnp.float32)
    attention = attention.astype(jnp.bfloat16).reshape(1, rows_dev, full_width)
    local_dprobs = jnp.einsum(
        "nqhd,nkhd->nhqk", grad_heads, local_values, preferred_element_type=jnp.float32
    )
    shared_dprobs = jnp.einsum(
        "nqhd,khd->nhqk", grad_heads, shared_values, preferred_element_type=jnp.float32
    )
    inner_sum = jnp.sum(local_probs * local_dprobs, axis=3, keepdims=True) + jnp.sum(
        shared_probs * shared_dprobs, axis=3, keepdims=True
    )
    local_dscores = (local_probs * (local_dprobs - inner_sum) * scaling).astype(jnp.bfloat16)
    shared_dscores = (shared_probs * (shared_dprobs - inner_sum) * scaling).astype(jnp.bfloat16)
    random_first = 3 * BLOCK
    random_last = (3 + R) * BLOCK
    local_terms = entry_terms(local_dscores, local_low, query_heads, grad_heads, 0, random_last)
    random_terms = (
        local_terms[:, random_first:random_last]
        .astype(jnp.bfloat16)
        .reshape(requests, BLOCK * pair_width)
    )
    window_part = local_terms[:, :random_first]
    slot_terms = jnp.dot(receive_hot.T, random_terms, preferred_element_type=jnp.float32).astype(
        jnp.bfloat16
    )
    returned_all = []
    for bit_index in range(bit_count):
        returned_all.append(
            partner(slot_terms[bit_index * capacity : (bit_index + 1) * capacity], "ctx", bit_index)
        )
    grad_queries = jnp.einsum(
        "nhqk,nkhd->nqhd", local_dscores, local_keys, preferred_element_type=jnp.float32
    ) + jnp.einsum(
        "nhqk,khd->nqhd", shared_dscores, shared_keys, preferred_element_type=jnp.float32
    )
    grad_queries = grad_queries.astype(jnp.bfloat16).reshape(1, rows_dev, full_width)
    window_terms = window_part.reshape(blocks_dev, 3, BLOCK, pair_width)
    left_terms = window_terms[:, 0]
    center_terms = window_terms[:, 1]
    right_terms = window_terms[:, 2]
    local_grads = (
        center_terms
        + jnp.pad(left_terms[1:], ((0, 1), (0, 0), (0, 0)))
        + jnp.pad(right_terms[:-1], ((1, 0), (0, 0), (0, 0)))
    )
    rim_out = jnp.concatenate([left_terms[0], right_terms[blocks_dev - 1]], axis=0).astype(
        jnp.bfloat16
    )
    rim_in = extended(rim_out, (("ctx", 0),), BLOCK).astype(jnp.float32)
    local_grads = local_grads.at[0].add(rim_in[0:BLOCK])
    local_grads = local_grads.at[blocks_dev - 1].add(rim_in[3 * BLOCK : 4 * BLOCK])
    local_grads = local_grads.reshape(blocks_dev, BLOCK * pair_width)
    for bit_index in range(bit_count):
        local_grads = local_grads + jnp.dot(
            send_tables[bit_index].T, returned_all[bit_index], preferred_element_type=jnp.float32
        )
    shared_key_terms = jnp.einsum(
        "nhqk,nqhd->khd", shared_dscores, query_heads, preferred_element_type=jnp.float32
    ).reshape(global_count, full_width)
    shared_value_terms = jnp.einsum(
        "nhqk,nqhd->khd", shared_low, grad_heads, preferred_element_type=jnp.float32
    ).reshape(global_count, full_width)
    global_terms = jnp.concatenate([shared_key_terms, shared_value_terms], axis=1)
    global_total = lax.psum(global_terms, ("ctx", "dp"))
    grad_pairs = local_grads.reshape(rows_dev, pair_width)
    grad_keys = grad_pairs[:, :full_width].astype(jnp.bfloat16)[None]
    grad_values = grad_pairs[:, full_width:].astype(jnp.bfloat16)[None]
    return (
        attention,
        grad_queries,
        grad_keys,
        grad_values,
        global_total[:, :full_width],
        global_total[:, full_width:],
    )


def solution(mesh):
    return jax.shard_map(
        body,
        mesh=mesh,
        in_specs=(
            P("dp", "ctx", None),
            P("dp", "ctx", None),
            P("dp", "ctx", None),
            P(),
            P(),
            P("dp", "ctx", None),
            P(),
            P(),
        ),
        out_specs=(
            P("dp", "ctx", None),
            P("dp", "ctx", None),
            P("dp", "ctx", None),
            P("dp", "ctx", None),
            P(),
            P(),
        ),
        check_vma=False,
    )
```

profile of v0, /device:TPU:1, one launch (start us, length us, event | category | flops | bytes accessed | tf_op | source)
XLA Modules:
  0.0 220.0 jit_solution(9830116949952567034)
XLA Ops:
  8.2 4.1 %collective-permute-start = (bf16[64,1024]{1,0:T(8,128)(2,1)S(1)}, bf16[64,1024]{1,0:T(8,128)(2,1)S(1)}, u32[]{:S(2)}, u32[]{:S(2)}) collective-permute-start(bf16[64,1024]{1,0:T(8,128)(2,1)S(1)} %get-tuple-element.48), channel_id=1, source_target_pairs={{0,4},{4,8},{8,12},{12,16},{16,20},{20,24},{24,28},{1,5},{5,9},{9,... | collective-permute-start | bytes 393224 | tf_op jit(solution)/shard_map/ppermute | solution.py:29
  12.3 1.3 collective-permute-start.1
  18.9 1.0 copy.152
  19.9 1.1 reshape_squeeze.6
  23.1 1.1 convolution_convert_fusion.3
  24.3 1.1 convolution_convert_fusion.4
  25.4 2.1 collective-permute-start.2
  27.5 1.3 collective-permute-start.3
  28.8 2.3 %collective-permute-start.4 = (bf16[2,65536]{1,0:T(2,128)(2,1)S(1)}, bf16[2,65536]{1,0:T(2,128)(2,1)}, u32[]{:S(2)}, u32[]{:S(2)}) collective-permute-start(bf16[2,65536]{1,0:T(2,128)(2,1)S(1)} %convolution_convert_fusion.2), channel_id=1, source_target_pairs={{0,16},{4,20},{8,24},{12,28},{16,0},{20,4},{24,8},{28,12},{1,17},{... | collective-permute-start | bytes 786440 | tf_op jit(solution)/shard_map/ppermute | solution.py:19
  33.8 5.4 %collective-permute-done.3 = bf16[2,65536]{1,0:T(2,128)(2,1)} collective-permute-done((bf16[2,65536]{1,0:T(2,128)(2,1)}, bf16[2,65536]{1,0:T(2,128)(2,1)}, u32[]{:S(2)}, u32[]{:S(2)}) %collective-permute-start.3) | collective-permute-done | bytes 262176 | tf_op jit(solution)/shard_map/ppermute | solution.py:19
  39.2 3.0 %convolution_convert_fusion.1 = bf16[6,65536]{1,0:T(8,128)(2,1)} fusion(bf16[2,65536]{1,0:T(2,128)(2,1)} %collective-permute-done.4, bf16[2,65536]{1,0:T(2,128)(2,1)} %collective-permute-done.3, bf16[2,65536]{1,0:T(2,128)(2,1)S(1)} %collective-permute-done.2, pred[6,2]{1,0:T(8,128)(4,1)S(1)} %fusion.38, pred[6,2]{1,0:T(8,128)(4,1)S(1)} %get-tuple-element.66, ...), kind=kOutput, calls=%fused_computation.1 | convolution fusion | flops 7471248 | bytes 1572900 | tf_op jit(solution)/shard_map/dot_general | solution.py:112
  42.3 2.4 %reshape.465 = bf16[2,192,1024]{2,1,0:T(8,128)(2,1)S(1)} reshape(bf16[6,65536]{1,0:T(8,128)(2,1)} %convolution_convert_fusion.1) | data formatting | bytes 1572864 | tf_op jit(solution)/shard_map/reshape | solution.py:115
  44.9 1.2 copy.149
  46.5 1.6 bitcast_reduce_fusion
  49.1 1.0 fusion.71
  50.2 1.7 fusion.26
  53.6 1.4 fusion.8
  55.0 1.9 copy.172
  56.9 2.6 %fusion.80 = f32[2,8,384,64]{2,3,1,0:T(8,128)} fusion(bf16[2,64,8,64]{1,3,2,0:T(8,128)(2,1)S(1)} %copy-done.15, bf16[2,8,64,384]{3,2,1,0:T(8,128)(2,1)} %fusion.8), kind=kOutput, calls=%fused_computation.159 | convolution fusion | flops 50331648 | bytes 2490368 | tf_op jit(solution)/shard_map/nhqk,nqhd->nkhd/dot_general | solution.py:57
  59.6 3.1 %copy.171 = f32[2,384,512]{2,1,0:T(8,128)} copy(f32[2,384,512]{1,2,0:T(8,128)} %bitcast.186) | data formatting | bytes 3145728 | tf_op jit(solution)/shard_map/reshape | solution.py:59
  62.6 2.3 %fusion.4 = bf16[2,192,1024]{2,1,0:T(8,128)(2,1)} fusion(f32[2,384,512]{2,1,0:T(8,128)S(1)} %copy.172, f32[2,384,512]{2,1,0:T(8,128)} %copy.171), kind=kLoop, calls=%fused_computation.13 | loop fusion | flops 1572864 | bytes 3932160 | tf_op jit(solution)/shard_map/convert.15
  67.7 2.4 %fusion.14 = bf16[2,64,8,64]{1,3,2,0:T(8,128)(2,1)} fusion(f32[2,64,8,64]{1,3,2,0:T(8,128)S(1)} %convolution_bitcast_fusion.2, bf16[2,384,8,64]{1,3,2,0:T(8,128)(2,1)} %bitcast.206, f32[2,8,384,64]{2,3,1,0:T(8,128)S(1)} %get-tuple-element.60, f32[2,8,64]{2,1,0:T(8,128)S(1)} %copy_add_fusion.1, f32[2,8,64]{2,1,0:T(8,128)S(1)} %copy_maximum_fusion), kind=kOutput, calls=%fused_computation.33 | convolution fusion | flops 51642368 | bytes 2760704 | tf_op jit(solution)/shard_map/nhqk,nkhd->nqhd/dot_general | solution.py:153
  70.2 1.2 copy.161
  78.6 1.4 collective-permute-start.7
  80.1 2.5 %collective-permute-start.9 = (bf16[2,65536]{1,0:T(2,128)(2,1)S(1)}, bf16[2,65536]{1,0:T(2,128)(2,1)S(1)}, u32[]{:S(2)}, u32[]{:S(2)}) collective-permute-start(bf16[2,65536]{1,0:T(2,128)(2,1)S(1)} %get-tuple-element.37), channel_id=1, source_target_pairs={{0,16},{4,20},{8,24},{12,28},{16,0},{20,4},{24,8},{28,12},{1,17},{... | collective-permute-start | bytes 786440 | tf_op jit(solution)/shard_map/ppermute | solution.py:19
  82.6 1.4 collective-permute-start.8
  85.0 2.2 collective-permute-start.5
  87.2 1.3 collective-permute-start.6
  88.5 1.1 fusion.22
  89.6 3.7 %collective-permute-done.6 = bf16[64,1024]{1,0:T(8,128)(2,1)S(1)} collective-permute-done((bf16[64,1024]{1,0:T(8,128)(2,1)S(1)}, bf16[64,1024]{1,0:T(8,128)(2,1)S(1)}, u32[]{:S(2)}, u32[]{:S(2)}) %collective-permute-start.6) | collective-permute-done | bytes 131104 | tf_op jit(solution)/shard_map/ppermute | solution.py:30
  93.9 114.7 %all-reduce.4.cloned.1.call-done = f32[128,1024]{1,0:T(8,128)} async-done(((f32[128,1024]{1,0:T(8,128)}), f32[128,1024]{1,0:T(8,128)}) %all-reduce.4.cloned.1.call-update) | async-done | bytes 524304 | tf_op jit(solution)/shard_map/psum | solution.py:218
  208.6 1.9 fusion.75
  (196 shorter events, 28.2 us)
Async XLA Ops:
  7.2 201.4 %all-reduce.4.cloned.1.call-start = ((), (), s32[]{:S(2)}) async-start(), calls=%async_computation | async-start | bytes 1048576 | tf_op jit(solution)/shard_map/psum | solution.py:218
  8.2 14.2 %copy-start.18 = (bf16[1,128,512]{2,1,0:T(8,128)(2,1)S(1)}, bf16[1,128,512]{2,1,0:T(8,128)(2,1)}, u32[]{:S(2)}) copy-start(bf16[1,128,512]{2,1,0:T(8,128)(2,1)} %param.13) | copy-start | bytes 393220
  8.2 14.2 %copy-start.19 = (bf16[1,128,512]{2,1,0:T(8,128)(2,1)S(1)}, bf16[1,128,512]{2,1,0:T(8,128)(2,1)}, u32[]{:S(2)}) copy-start(bf16[1,128,512]{2,1,0:T(8,128)(2,1)} %param.14) | copy-start | bytes 393220
  8.2 14.2 %collective-permute-start = (bf16[64,1024]{1,0:T(8,128)(2,1)S(1)}, bf16[64,1024]{1,0:T(8,128)(2,1)S(1)}, u32[]{:S(2)}, u32[]{:S(2)}) collective-permute-start(bf16[64,1024]{1,0:T(8,128)(2,1)S(1)} %get-tuple-element.48), channel_id=1, source_target_pairs={{0,4},{4,8},{8,12},{12,16},{16,20},{20,24},{24,28},{1,5},{5,9},{9,... | collective-permute-start | bytes 393224 | tf_op jit(solution)/shard_map/ppermute | solution.py:29
  12.3 10.1 %collective-permute-start.1 = (bf16[64,1024]{1,0:T(8,128)(2,1)S(1)}, bf16[64,1024]{1,0:T(8,128)(2,1)S(1)}, u32[]{:S(2)}, u32[]{:S(2)}) collective-permute-start(bf16[64,1024]{1,0:T(8,128)(2,1)S(1)} %get-tuple-element.49), channel_id=1, source_target_pairs={{4,0},{8,4},{12,8},{16,12},{20,16},{24,20},{28,24},{5,1},{9,5},{13... | collective-permute-start | bytes 393224 | tf_op jit(solution)/shard_map/ppermute | solution.py:30
  21.0 10.3 %copy-start.9 = (bf16[2,64,8,64]{3,2,1,0:T(8,128)(2,1)}, bf16[2,64,8,64]{3,2,1,0:T(8,128)(2,1)S(1)}, u32[]{:S(2)}) copy-start(bf16[2,64,8,64]{3,2,1,0:T(8,128)(2,1)S(1)} %reshape_squeeze.6) | copy-start | bytes 393220
  21.2 18.1 %copy-start.26 = (pred[6,2]{1,0:T(8,128)(4,1)}, pred[6,2]{1,0:T(8,128)(4,1)S(1)}, u32[]{:S(2)}) copy-start(pred[6,2]{1,0:T(8,128)(4,1)S(1)} %fusion.38) | copy-start | bytes 40
  21.6 2.6 %copy-start.32 = (bf16[2,2]{1,0:T(2,128)(2,1)}, bf16[2,2]{1,0:T(2,128)(2,1)S(1)}, u32[]{:S(2)}) copy-start(bf16[2,2]{1,0:T(2,128)(2,1)S(1)} %convolution_convert_fusion.7) | copy-start | bytes 28
  22.1 17.1 %copy-start.28 = (pred[6,2]{1,0:T(8,128)(4,1)}, pred[6,2]{1,0:T(8,128)(4,1)S(1)}, u32[]{:S(2)}) copy-start(pred[6,2]{1,0:T(8,128)(4,1)S(1)} %get-tuple-element.65) | copy-start | bytes 40
  22.1 17.1 %copy-start.30 = (pred[6,2]{1,0:T(8,128)(4,1)}, pred[6,2]{1,0:T(8,128)(4,1)S(1)}, u32[]{:S(2)}) copy-start(pred[6,2]{1,0:T(8,128)(4,1)S(1)} %get-tuple-element.66) | copy-start | bytes 40
  23.1 9.1 %copy-start.24 = (bf16[1,128,512]{2,1,0:T(8,128)(2,1)S(1)}, bf16[1,128,512]{2,1,0:T(8,128)(2,1)}, u32[]{:S(2)}) copy-start(bf16[1,128,512]{2,1,0:T(8,128)(2,1)} %param.17) | copy-start | bytes 393220
  24.3 9.1 %copy-start.25 = (bf16[128,512]{1,0:T(8,128)(2,1)S(1)}, bf16[128,512]{1,0:T(8,128)(2,1)}, u32[]{:S(2)}) copy-start(bf16[128,512]{1,0:T(8,128)(2,1)} %param.16) | copy-start | bytes 393220
  25.4 8.4 %collective-permute-start.2 = (bf16[2,65536]{1,0:T(2,128)(2,1)}, bf16[2,65536]{1,0:T(2,128)(2,1)S(1)}, u32[]{:S(2)}, u32[]{:S(2)}) collective-permute-start(bf16[2,65536]{1,0:T(2,128)(2,1)} %convolution_convert_fusion.4), channel_id=1, source_target_pairs={{0,4},{4,0},{8,12},{12,8},{16,20},{20,16},{24,28},{28,24},{1,5},{5... | collective-permute-start | bytes 786440 | tf_op jit(solution)/shard_map/ppermute | solution.py:19
  27.5 11.7 %collective-permute-start.3 = (bf16[2,65536]{1,0:T(2,128)(2,1)}, bf16[2,65536]{1,0:T(2,128)(2,1)}, u32[]{:S(2)}, u32[]{:S(2)}) collective-permute-start(bf16[2,65536]{1,0:T(2,128)(2,1)} %convolution_convert_fusion.3), channel_id=1, source_target_pairs={{0,8},{4,12},{8,0},{12,4},{16,24},{20,28},{24,16},{28,20},{1,9},{5... | collective-permute-start | bytes 786440 | tf_op jit(solution)/shard_map/ppermute | solution.py:19
  28.8 10.4 %collective-permute-start.4 = (bf16[2,65536]{1,0:T(2,128)(2,1)S(1)}, bf16[2,65536]{1,0:T(2,128)(2,1)}, u32[]{:S(2)}, u32[]{:S(2)}) collective-permute-start(bf16[2,65536]{1,0:T(2,128)(2,1)S(1)} %convolution_convert_fusion.2), channel_id=1, source_target_pairs={{0,16},{4,20},{8,24},{12,28},{16,0},{20,4},{24,8},{28,12},{1,17},{... | collective-permute-start | bytes 786440 | tf_op jit(solution)/shard_map/ppermute | solution.py:19
  32.4 9.8 %copy-start.11 = (bf16[2,64,8,64]{3,2,1,0:T(8,128)(2,1)}, bf16[2,64,8,64]{3,2,1,0:T(8,128)(2,1)S(1)}, u32[]{:S(2)}) copy-start(bf16[2,64,8,64]{3,2,1,0:T(8,128)(2,1)S(1)} %reshape_squeeze.7) | copy-start | bytes 393220
  33.5 5.7 %copy-start.16 = (bf16[128,512]{0,1:T(8,128)(2,1)}, bf16[128,512]{0,1:T(8,128)(2,1)S(1)}, u32[]{:S(2)}) copy-start(bf16[128,512]{0,1:T(8,128)(2,1)S(1)} %copy.158) | copy-start | bytes 393220
  33.7 19.0 %copy-start.5 = (f32[8,128,128]{1,2,0}, f32[8,128,128]{1,2,0:S(1)}, u32[]{:S(2)}) copy-start(f32[8,128,128]{1,2,0:S(1)} %fusion.79) | copy-start | bytes 1572868
  50.2 2.6 %copy-start.7 = (f32[2,8,64,128]{3,2,0,1:T(8,128)}, f32[2,8,64,128]{3,2,0,1:T(8,128)S(1)}, u32[]{:S(2)}) copy-start(f32[2,8,64,128]{3,2,0,1:T(8,128)S(1)} %get-tuple-element.31) | copy-start | bytes 1572868
  67.7 4.5 %copy-start.6 = (f32[8,128,128]{1,2,0:S(1)}, f32[8,128,128]{1,2,0}, u32[]{:S(2)}) copy-start(f32[8,128,128]{1,2,0} %copy-done.5) | copy-start | bytes 1572868
  67.7 4.5 %copy-start.8 = (f32[2,8,64,128]{3,2,0,1:T(8,128)S(1)}, f32[2,8,64,128]{3,2,0,1:T(8,128)}, u32[]{:S(2)}) copy-start(f32[2,8,64,128]{3,2,0,1:T(8,128)} %copy-done.7) | copy-start | bytes 1572868
  70.2 3.0 %copy-start.10 = (bf16[2,64,8,64]{3,2,1,0:T(8,128)(2,1)S(1)}, bf16[2,64,8,64]{3,2,1,0:T(8,128)(2,1)}, u32[]{:S(2)}) copy-start(bf16[2,64,8,64]{3,2,1,0:T(8,128)(2,1)} %copy-done.9) | copy-start | bytes 393220
  78.0 10.4 %copy-start.20 = (f32[1,64,1024]{2,1,0:T(8,128)S(1)}, f32[1,64,1024]{2,1,0:T(8,128)}, u32[]{:S(2)}) copy-start(f32[1,64,1024]{2,1,0:T(8,128)} %get-tuple-element.32) | copy-start | bytes 786436
  78.1 10.4 %copy-start.21 = (f32[1,64,1024]{2,1,0:T(8,128)S(1)}, f32[1,64,1024]{2,1,0:T(8,128)}, u32[]{:S(2)}) copy-start(f32[1,64,1024]{2,1,0:T(8,128)} %get-tuple-element.33) | copy-start | bytes 786436
  78.6 132.8 %collective-permute-start.7 = (bf16[2,65536]{1,0:T(2,128)(2,1)S(1)}, bf16[2,65536]{1,0:T(2,128)(2,1)S(1)}, u32[]{:S(2)}, u32[]{:S(2)}) collective-permute-start(bf16[2,65536]{1,0:T(2,128)(2,1)S(1)} %get-tuple-element.36), channel_id=1, source_target_pairs={{0,4},{4,0},{8,12},{12,8},{16,20},{20,16},{24,28},{28,24},{1,5},{5... | collective-permute-start | bytes 786440 | tf_op jit(solution)/shard_map/ppermute | solution.py:19
  80.1 130.4 %collective-permute-start.9 = (bf16[2,65536]{1,0:T(2,128)(2,1)S(1)}, bf16[2,65536]{1,0:T(2,128)(2,1)S(1)}, u32[]{:S(2)}, u32[]{:S(2)}) collective-permute-start(bf16[2,65536]{1,0:T(2,128)(2,1)S(1)} %get-tuple-element.37), channel_id=1, source_target_pairs={{0,16},{4,20},{8,24},{12,28},{16,0},{20,4},{24,8},{28,12},{1,17},{... | collective-permute-start | bytes 786440 | tf_op jit(solution)/shard_map/ppermute | solution.py:19
  82.6 128.4 %collective-permute-start.8 = (bf16[2,65536]{1,0:T(2,128)(2,1)S(1)}, bf16[2,65536]{1,0:T(2,128)(2,1)S(1)}, u32[]{:S(2)}, u32[]{:S(2)}) collective-permute-start(bf16[2,65536]{1,0:T(2,128)(2,1)S(1)} %get-tuple-element.38), channel_id=1, source_target_pairs={{0,8},{4,12},{8,0},{12,4},{16,24},{20,28},{24,16},{28,20},{1,9},{5... | collective-permute-start | bytes 786440 | tf_op jit(solution)/shard_map/ppermute | solution.py:19
  85.0 4.6 %collective-permute-start.5 = (bf16[64,1024]{1,0:T(8,128)(2,1)S(1)}, bf16[64,1024]{1,0:T(8,128)(2,1)S(1)}, u32[]{:S(2)}, u32[]{:S(2)}) collective-permute-start(bf16[64,1024]{1,0:T(8,128)(2,1)S(1)} %get-tuple-element.39), channel_id=1, source_target_pairs={{0,4},{4,8},{8,12},{12,16},{16,20},{20,24},{24,28},{1,5},{5,9},{9,... | collective-permute-start | bytes 393224 | tf_op jit(solution)/shard_map/ppermute | solution.py:29
  87.2 6.2 %collective-permute-start.6 = (bf16[64,1024]{1,0:T(8,128)(2,1)S(1)}, bf16[64,1024]{1,0:T(8,128)(2,1)S(1)}, u32[]{:S(2)}, u32[]{:S(2)}) collective-permute-start(bf16[64,1024]{1,0:T(8,128)(2,1)S(1)} %get-tuple-element.40), channel_id=1, source_target_pairs={{4,0},{8,4},{12,8},{16,12},{20,16},{24,20},{28,24},{5,1},{9,5},{13... | collective-permute-start | bytes 393224 | tf_op jit(solution)/shard_map/ppermute | solution.py:30
  93.4 117.1 %copy-start.35 = (bf16[2,2]{1,0:T(2,128)(2,1)S(1)}, bf16[2,2]{1,0:T(2,128)(2,1)}, u32[]{:S(2)}) copy-start(bf16[2,2]{1,0:T(2,128)(2,1)} %copy-done.34) | copy-start | bytes 28
  93.5 117.5 %copy-start.37 = (bf16[2,2]{1,0:T(2,128)(2,1)S(1)}, bf16[2,2]{1,0:T(2,128)(2,1)}, u32[]{:S(2)}) copy-start(bf16[2,2]{1,0:T(2,128)(2,1)} %copy-done.36) | copy-start | bytes 28
  93.9 117.6 %copy-start.33 = (bf16[2,2]{1,0:T(2,128)(2,1)S(1)}, bf16[2,2]{1,0:T(2,128)(2,1)}, u32[]{:S(2)}) copy-start(bf16[2,2]{1,0:T(2,128)(2,1)} %copy-done.32) | copy-start | bytes 28
  (17 other events, 31.7 us)
Sparse Core Ops, SparseCore 0:
  74.5 134.0 all-reduce.3
where the time goes:
time: 222 us; the launch traced here: 220 us
  waiting for transfers between devices  124 us (56%)
  local copies, waits for them, and re-layouts  27.7 us (12%)
  matrix products  20 us (9%)
  starting transfers between devices  19.9 us (9%)
  between operations  14.9 us (7%)
  other arithmetic  13.6 us (6%)
    psum x1, waiting for transfers between devices, body(): global_total = lax.psum(global_terms, ('ctx', 'dp'))  115 us
    ppermute x6, starting transfers between devices, partner(): return lax.ppermute(value, axis, pairs)  11 us
    ppermute x2, starting transfers between devices, extended(): before = lax.ppermute(last, axis, up)  6.27 us
    ppermute x6, waiting for transfers between devices, partner(): return lax.ppermute(value, axis, pairs)  5.45 us
  transfers between devices with their start and end apart: 11, of which 3 were waited for; matrix products, arithmetic and copies ran while one was open for 9% of the time, Pallas kernels for 0%

commit v1 on v0

v1 whole, which is shorter than its diff:
```python
import functools
import math

import jax
import jax.numpy as jnp
from jax import lax
from jax.experimental import pallas as pl
from jax.experimental.pallas import tpu as pltpu
from jax.sharding import PartitionSpec as P

HEAD_DIM = 64
BLOCK = 64
R = 3
LANES = 128
MASKED = -1e30
MESH = pl.DeviceIdType.MESH
NT = (((1,), (1,)), ((), ()))
TN = (((0,), (0,)), ((), ()))


def reduce_stages(sizes, rows):
    stages = []
    for axis, size in sizes:
        stride = 1
        while stride < size:
            radix = min(8, size // stride)
            if rows % (radix * 16) == 0:
                rows //= radix
            stages.append((axis, stride, radix, rows))
            stride *= radix
    return stages


def kernel(
    shards, stages, q_ref, k_ref, v_ref, gk_ref, gv_ref, u_ref, ps_ref, pb_ref,
    att_ref, dq_ref, dk_ref, dv_ref, dgk_ref, dgv_ref,
    kv, bias, terms, back, own, *rest,
):
    count = len(stages)
    accs, recvs = rest[:count], rest[count : 2 * count]
    final = rest[2 * count]
    kv_send, kv_recv, t_send, t_recv = rest[2 * count + 1 : 2 * count + 5]
    sems = rest[2 * count + 5 :]
    rs_send, rs_recv = sems[:count], sems[count : 2 * count]
    ag_send, ag_recv = sems[2 * count : 3 * count], sems[3 * count :]

    rows, width = q_ref.shape
    blocks = rows // BLOCK
    chunks = width // LANES
    bits = shards.bit_length() - 1
    globals_ = gk_ref.shape[0]
    edge_at = rows * (1 + bits)
    glob_at = edge_at + BLOCK
    total = kv.shape[2]
    me = lax.axis_index("ctx")
    spot = {"ctx": me, "dp": lax.axis_index("dp")}
    odd = lax.rem(me, 2)
    edge_peer = me - 1 + 2 * odd
    has_edge = jnp.logical_and(edge_peer >= 0, edge_peer < shards)
    edge_first = pl.multiple_of(odd * (rows - BLOCK), BLOCK)
    peers = [me + (1 << b) * (1 - 2 * lax.rem(lax.div(me, 1 << b), 2)) for b in range(bits)]

    barrier = pltpu.get_barrier_semaphore()

    def greet(axis, to):
        pl.semaphore_signal(barrier, inc=1, device_id={axis: to}, device_id_type=MESH)

    greeted = 0
    for axis, stride, radix, _ in stages:
        digit = lax.rem(lax.div(spot[axis], stride), radix)
        for k in range(1, radix):
            greet(axis, spot[axis] + (lax.rem(digit + k, radix) - digit) * stride)
            greeted += 1

    apart = all(radix < shards for axis, _, radix, _ in stages if axis == "ctx")
    if apart:

        @pl.when(has_edge)
        def _():
            greet("ctx", edge_peer)

    for c in range(chunks):
        lanes = slice(c * LANES, (c + 1) * LANES)
        kv[c, 0, 0:rows] = k_ref[:, lanes]
        kv[c, 1, 0:rows] = v_ref[:, lanes]

    pl.semaphore_wait(barrier, greeted + jnp.where(has_edge, 1, 0) if apart else greeted)

    def kv_copy(c, b):
        return pltpu.make_async_remote_copy(
            src_ref=kv.at[c, :, pl.ds(0, rows)],
            dst_ref=kv.at[c, :, pl.ds(rows * (1 + b), rows)],
            send_sem=kv_send.at[c, b], recv_sem=kv_recv.at[c, b],
            device_id={"ctx": peers[b]}, device_id_type=MESH,
        )

    def kv_edge(c):
        return pltpu.make_async_remote_copy(
            src_ref=kv.at[c, :, pl.ds(edge_first, BLOCK)],
            dst_ref=kv.at[c, :, pl.ds(edge_at, BLOCK)],
            send_sem=kv_send.at[c, bits], recv_sem=kv_recv.at[c, bits],
            device_id={"ctx": edge_peer}, device_id_type=MESH,
        )

    def term_copy(c, b):
        return pltpu.make_async_remote_copy(
            src_ref=terms.at[c, :, pl.ds(rows * b, rows)],
            dst_ref=back.at[c, :, pl.ds(rows * b, rows)],
            send_sem=t_send.at[c, b], recv_sem=t_recv.at[c, b],
            device_id={"ctx": peers[b]}, device_id_type=MESH,
        )

    def term_edge(c):
        return pltpu.make_async_remote_copy(
            src_ref=terms.at[c, :, pl.ds(rows * bits, BLOCK)],
            dst_ref=back.at[c, :, pl.ds(rows * bits, BLOCK)],
            send_sem=t_send.at[c, bits], recv_sem=t_recv.at[c, bits],
            device_id={"ctx": edge_peer}, device_id_type=MESH,
        )

    order = list(range(bits))[::-1]
    for c in range(chunks):
        for b in order:
            kv_copy(c, b).start()

        @pl.when(has_edge)
        def _():
            kv_edge(c).start()

    for c in range(chunks):
        lanes = slice(c * LANES, (c + 1) * LANES)
        kv[c, 0, glob_at : glob_at + globals_] = gk_ref[:, lanes]
        kv[c, 1, glob_at : glob_at + globals_] = gv_ref[:, lanes]
        if total > glob_at + globals_:
            kv[c, :, glob_at + globals_ :] = jnp.zeros(
                (2, total - glob_at - globals_, LANES), kv.dtype
            )

    @pl.when(jnp.logical_not(has_edge))
    def _():
        kv[:, :, edge_at : edge_at + BLOCK] = jnp.zeros((chunks, 2, BLOCK, LANES), kv.dtype)
        back[:, :, rows * bits : rows * bits + BLOCK] = jnp.zeros(
            (chunks, 2, BLOCK, LANES), back.dtype
        )

    pair = 2 * rows
    query_block = lax.rem(lax.div(lax.broadcasted_iota(jnp.int32, (8, pair), 1), BLOCK), blocks)
    first_block = me * blocks
    listed = [
        [(ps_ref[first_block + n, r], pb_ref[first_block + n, r]) for r in range(R)]
        for n in range(blocks)
    ]

    def put_bias(at, counts):
        times = jnp.zeros((8, pair), jnp.int32)
        for n in range(blocks):
            times = jnp.where(query_block == n, counts[n], times)
        times = times.astype(jnp.float32)
        line = jnp.where(times > 0.5, jnp.log(jnp.maximum(times, 1.0)), MASKED)
        for step in range(BLOCK // 8):
            bias[at + step * 8 : at + step * 8 + 8] = line

    for j in range(blocks):
        put_bias(j * BLOCK, [jnp.int32(1 if abs(j - n) <= 1 else 0) for n in range(blocks)])
    for b in range(bits):
        for j in range(blocks):
            counts = []
            for n in range(blocks):
                times = jnp.int32(0)
                for shard, block in listed[n]:
                    times += jnp.where(shard == peers[b], 1, 0) * jnp.where(block == j, 1, 0)
                if b == 0 and j == 0 and n == blocks - 1:
                    times += 1 - odd
                if b == 0 and j == blocks - 1 and n == 0:
                    times += odd
                counts.append(times)
            put_bias(rows * (1 + b) + j * BLOCK, counts)
    valid = jnp.where(has_edge, 1, 0)
    edge_counts = [jnp.int32(0)] * blocks
    edge_counts[0] = edge_counts[0] + (1 - odd) * valid
    edge_counts[blocks - 1] = edge_counts[blocks - 1] + odd * valid
    put_bias(edge_at, edge_counts)
    for at in range(glob_at, glob_at + globals_, BLOCK):
        put_bias(at, [jnp.int32(1)] * blocks)
    if total > glob_at + globals_:
        bias[glob_at + globals_ :] = jnp.full((total - glob_at - globals_, pair), MASKED)

    low_head = lax.broadcasted_iota(jnp.int32, (rows, LANES), 1) < HEAD_DIM
    scaling = 1.0 / math.sqrt(HEAD_DIM)

    def both_heads(x):
        x = x.astype(jnp.float32)
        zero = jnp.zeros_like(x)
        return jnp.concatenate(
            [jnp.where(low_head, x, zero), jnp.where(low_head, zero, x)], axis=0
        )

    def dot(a, b, dims):
        return lax.dot_general(a, b, dims, preferred_element_type=jnp.float32)

    NN = (((1,), (0,)), ((), ()))

    def step(c, carry):
        lanes = pl.ds(pl.multiple_of(c * LANES, LANES), LANES)
        queries = (both_heads(q_ref[:, lanes]) * scaling).astype(jnp.bfloat16)
        grads = both_heads(u_ref[:, lanes]).astype(jnp.bfloat16)
        for b in order:
            kv_copy(c, b).wait_recv()

        @pl.when(has_edge)
        def _():
            kv_edge(c).wait_recv()

        keys = kv[c, 0]
        values = kv[c, 1]
        scores = dot(keys, queries, NT) + bias[...]
        weights = jnp.exp(scores - jnp.max(scores, axis=0, keepdims=True))
        probs = weights * (1.0 / jnp.sum(weights, axis=0, keepdims=True))
        low = probs.astype(jnp.bfloat16)
        dprobs = dot(values, grads, NT)
        inner = jnp.sum(probs * dprobs, axis=0, keepdims=True)
        dscores = (probs * (dprobs - inner)).astype(jnp.bfloat16)
        for which, (left, right) in enumerate(((dscores, queries), (low, grads))):
            made = dot(left, right, NN)
            own[c, which] = made[0:rows]
            terms[c, which] = made[rows:glob_at].astype(jnp.bfloat16)
            accs[0][
                pl.ds(pl.multiple_of((c * 2 + which) * globals_, globals_), globals_)
            ] = made[glob_at : glob_at + globals_].astype(jnp.bfloat16)
        for b in order:
            term_copy(c, b).start()

        @pl.when(has_edge)
        def _():
            term_edge(c).start()

        attention = dot(low, values, TN)
        att_ref[:, lanes] = jnp.where(low_head, attention[:rows], attention[rows:]).astype(
            jnp.bfloat16
        )
        dqueries = dot(dscores, keys, TN)
        dq_ref[:, lanes] = (
            jnp.where(low_head, dqueries[:rows], dqueries[rows:]) * scaling
        ).astype(jnp.bfloat16)
        return carry

    lax.fori_loop(0, chunks, step, 0)

    def digit_of(i):
        axis, stride, radix, _ = stages[i]
        return lax.rem(lax.div(spot[axis], stride), radix)

    def peer_of(i, k):
        axis, stride, radix, _ = stages[i]
        digit = digit_of(i)
        other = lax.rem(digit + k, radix)
        return other, {axis: spot[axis] + (other - digit) * stride}

    def scatter_copy(i, k):
        held = stages[i][3]
        other, device = peer_of(i, k)
        at = other * held if accs[i].shape[0] != held else 0
        return pltpu.make_async_remote_copy(
            src_ref=accs[i].at[pl.ds(pl.multiple_of(at, 16), held)],
            dst_ref=recvs[i].at[k - 1],
            send_sem=rs_send[i].at[k - 1], recv_sem=rs_recv[i].at[k - 1],
            device_id=device, device_id_type=MESH,
        )

    starts = []
    start = 0
    for i, (axis, stride, radix, held) in enumerate(stages):
        if accs[i].shape[0] != held:
            start = start + digit_of(i) * held
        starts.append(start)

    def scatter_start(i):
        for k in range(1, stages[i][2]):
            scatter_copy(i, k).start()

    def scatter_end(i):
        held = stages[i][3]
        at = digit_of(i) * held if accs[i].shape[0] != held else 0
        summed = accs[i][pl.ds(pl.multiple_of(at, 16), held)].astype(jnp.float32)
        for k in range(1, stages[i][2]):
            scatter_copy(i, k).wait_recv()
            summed = summed + recvs[i][k - 1].astype(jnp.float32)
        summed = summed.astype(jnp.bfloat16)
        if i + 1 < count:
            accs[i + 1][...] = summed
        else:
            final[pl.ds(pl.multiple_of(starts[i], 16), held)] = summed

    def gather_copy(i, k, at):
        held = stages[i][3]
        part = final.at[pl.ds(pl.multiple_of(at, 16), held)]
        return pltpu.make_async_remote_copy(
            src_ref=part, dst_ref=part,
            send_sem=ag_send[i].at[k - 1], recv_sem=ag_recv[i].at[k - 1],
            device_id=peer_of(i, k)[1], device_id_type=MESH,
        )

    def gather_start(i):
        for k in range(1, stages[i][2]):
            gather_copy(i, k, starts[i]).start()

    def gather_end(i):
        _, _, radix, held = stages[i]
        for k in range(1, radix):
            behind = lax.rem(digit_of(i) + radix - k, radix)
            gather_copy(i, k, starts[i] + (behind - digit_of(i)) * held).wait_recv()

    def collect(c):
        lanes = slice(c * LANES, (c + 1) * LANES)
        for b in order:
            term_copy(c, b).wait_recv()

        @pl.when(has_edge)
        def _():
            term_edge(c).wait_recv()

        low_rows = lax.broadcasted_iota(jnp.int32, (rows, LANES), 0)
        at_edge = jnp.logical_and(low_rows >= edge_first, low_rows < edge_first + BLOCK)
        for which, out in enumerate((dk_ref, dv_ref)):
            summed = own[c, which]
            for b in range(bits):
                summed = summed + back[c, which, rows * b : rows * (b + 1)].astype(jnp.float32)
            edge = back[c, which, rows * bits : rows * bits + BLOCK].astype(jnp.float32)
            edge = jnp.concatenate([edge] * blocks, axis=0)
            summed = summed + jnp.where(at_edge, edge, 0.0)
            out[:, lanes] = summed.astype(jnp.bfloat16)

    for i in range(count):
        scatter_start(i)
        scatter_end(i)
    split = [i for i in range(count) if accs[i].shape[0] != stages[i][3]]
    todo = list(range(chunks))
    for i in split[::-1]:
        gather_start(i)
        if todo:
            collect(todo.pop(0))
        gather_end(i)
    for c in range(chunks):
        lanes = slice(c * LANES, (c + 1) * LANES)
        for which, out in enumerate((dgk_ref, dgv_ref)):
            at = (c * 2 + which) * globals_
            out[:, lanes] = final[at : at + globals_].astype(jnp.float32)
    for c in todo:
        collect(c)

    for c in range(chunks):
        for b in order:
            kv_copy(c, b).wait_send()
            term_copy(c, b).wait_send()

        @pl.when(has_edge)
        def _():
            kv_edge(c).wait_send()
            term_edge(c).wait_send()

    for i in range(count):
        for k in range(1, stages[i][2]):
            scatter_copy(i, k).wait_send()
            if i in split:
                gather_copy(i, k, starts[i]).wait_send()


def body(shards, replicas, queries, keys, values, global_keys, global_values, upstream, ps, pb):
    _, rows, width = queries.shape
    globals_ = global_keys.shape[0]
    bits = shards.bit_length() - 1
    chunks = width // LANES
    used = rows * (1 + bits) + BLOCK + globals_
    total = -(-used // LANES) * LANES
    gathered = 2 * chunks * globals_
    stages = reduce_stages((("dp", replicas), ("ctx", shards)), gathered)
    low = jnp.bfloat16
    accs, recvs, sems = [], [], []
    held = gathered
    for _, _, radix, after in stages:
        accs.append(pltpu.VMEM((held, LANES), low))
        recvs.append(pltpu.VMEM((radix - 1, after, LANES), low))
        sems.append(pltpu.SemaphoreType.DMA((radix - 1,)))
        held = after
    vmem = pl.BlockSpec(memory_space=pltpu.VMEM)
    smem = pl.BlockSpec(memory_space=pltpu.SMEM)
    dma = pltpu.SemaphoreType.DMA((chunks, bits + 1))
    remote = rows * bits + BLOCK
    outs = pl.pallas_call(
        functools.partial(kernel, shards, stages),
        out_shape=[jax.ShapeDtypeStruct((rows, width), low)] * 4
        + [jax.ShapeDtypeStruct((globals_, width), jnp.float32)] * 2,
        in_specs=[vmem] * 6 + [smem] * 2,
        out_specs=[vmem] * 6,
        scratch_shapes=[
            pltpu.VMEM((chunks, 2, total, LANES), low),
            pltpu.VMEM((total, 2 * rows), jnp.float32),
            pltpu.VMEM((chunks, 2, remote, LANES), low),
            pltpu.VMEM((chunks, 2, remote, LANES), low),
            pltpu.VMEM((chunks, 2, rows, LANES), jnp.float32),
            *accs,
            *recvs,
            pltpu.VMEM((gathered, LANES), low),
            dma, dma, dma, dma,
            *sems, *sems, *sems, *sems,
        ],
        compiler_params=pltpu.CompilerParams(
            collective_id=0, has_side_effects=True, vmem_limit_bytes=40 * 1024 * 1024
        ),
    )(queries[0], keys[0], values[0], global_keys, global_values, upstream[0], ps, pb)
    return (outs[0][None], outs[1][None], outs[2][None], outs[3][None], outs[4], outs[5])


def solution(mesh):
    split = P("dp", "ctx", None)
    return jax.shard_map(
        functools.partial(body, mesh.shape["ctx"], mesh.shape["dp"]),
        mesh=mesh,
        in_specs=(split, split, split, P(), P(), split, P(), P()),
        out_specs=(split, split, split, split, P(), P()),
        check_vma=False,
    )
```

time: 222 us -> 58.7 us (0.26)
  waiting for transfers between devices: 124 us -> 0 us
  Pallas kernels: 0 us -> 46.8 us
  matrix products: 20 us -> 0 us
  starting transfers between devices: 19.9 us -> 0 us
  local copies, waits for them, and re-layouts: 27.7 us -> 10.9 us
  between operations: 14.9 us -> 0.66 us
  other arithmetic: 13.6 us -> 0 us
    psum x1 -> x0, waiting for transfers between devices: 115 us -> none  [body(): global_total = lax.psum(global_terms, ('ctx', 'dp'))]
    pallas_call x0 -> x1, Pallas kernels: none -> 46.8 us  [body(): pl.pallas_call(functools.partial(kernel, shards, stages), out_shape=[jax....]
    ppermute x10 -> x0, starting transfers between devices: 19.9 us -> none  [the longest x6 11 us: partner(): return lax.ppermute(value, axis, pairs)]
    dot_general x21 -> x0, matrix products: 19.6 us -> none  [the longest x1 3.02 us: body(): jnp.dot(receive_hot, gathered, preferred_element_type=jnp.float32)]
    reshape x9 -> x0, local copies, waits for them, and re-layouts: 10.6 us -> none  [the longest x1 3.06 us: entry_terms(): key_terms = jnp.einsum('nhqk,nqhd->nkhd', grad_scores, query_heads, prefe...]
    ppermute x10 -> x0, waiting for transfers between devices: 9.16 us -> none  [the longest x6 5.45 us: partner(): return lax.ppermute(value, axis, pairs)]
    unnamed x79 -> x24, local copies, waits for them, and re-layouts: 1.88 us -> 10.9 us
    slice x6 -> x0, local copies, waits for them, and re-layouts: 4.9 us -> none  [the longest x1 1.85 us: body(): global_total[:, full_width:]]
  transfers between devices with their start and end apart: 11 -> 0, of which waited for: 3 -> 0; matrix products, arithmetic and copies ran while one was open for 9% -> 0% of each run, Pallas kernels for 0% -> 0%
where the time goes in v1:
time: 58.7 us; the launch traced here: 58.4 us
  Pallas kernels  46.8 us (80%)
  local copies, waits for them, and re-layouts  10.9 us (19%)
  between operations  0.66 us (1%)
    pallas_call x1, Pallas kernels, body(): pl.pallas_call(functools.partial(kernel, shards, stages), out_shape=[jax....  46.8 us
    unnamed x24, local copies, waits for them, and re-layouts  10.9 us

profile of v1, /device:TPU:1, one launch (start us, length us, event | category | flops | bytes accessed | tf_op | source)
XLA Modules:
  0.0 58.4 jit_solution(12078448095955571682)
XLA Ops:
  0.6 0.0 copy-start.6
  0.6 0.7 %copy-done.6 = s32[16,3]{0,1:T(4,128)S(1)} copy-done((s32[16,3]{0,1:T(4,128)S(1)}, s32[16,3]{0,1:T(4,128)}, u32[]{:S(2)}) %copy-start.6) | copy-done | bytes 216
  1.3 0.0 copy-start.7
  1.3 0.1 copy.14.ps_ref
  1.4 0.6 %copy-done.7 = s32[16,3]{0,1:T(4,128)S(1)} copy-done((s32[16,3]{0,1:T(4,128)S(1)}, s32[16,3]{0,1:T(4,128)}, u32[]{:S(2)}) %copy-start.7) | copy-done | bytes 216
  2.0 0.1 copy.15.pb_ref
  2.1 0.0 copy-start
  2.1 0.9 %copy-done = bf16[1,128,512]{2,1,0:T(8,128)(2,1)S(1)} copy-done((bf16[1,128,512]{2,1,0:T(8,128)(2,1)S(1)}, bf16[1,128,512]{2,1,0:T(8,128)(2,1)}, u32[]{:S(2)}) %copy-start) | copy-done | bytes 131096
  3.0 0.0 copy-start.1
  3.0 0.9 %copy-done.1 = bf16[1,128,512]{2,1,0:T(8,128)(2,1)S(1)} copy-done((bf16[1,128,512]{2,1,0:T(8,128)(2,1)S(1)}, bf16[1,128,512]{2,1,0:T(8,128)(2,1)}, u32[]{:S(2)}) %copy-start.1) | copy-done | bytes 131096
  3.9 0.0 copy-start.2
  3.9 0.9 %copy-done.2 = bf16[1,128,512]{2,1,0:T(8,128)(2,1)S(1)} copy-done((bf16[1,128,512]{2,1,0:T(8,128)(2,1)S(1)}, bf16[1,128,512]{2,1,0:T(8,128)(2,1)}, u32[]{:S(2)}) %copy-start.2) | copy-done | bytes 131096
  4.8 0.0 copy-start.3
  4.8 0.9 %copy-done.3 = bf16[128,512]{1,0:T(8,128)(2,1)S(1)} copy-done((bf16[128,512]{1,0:T(8,128)(2,1)S(1)}, bf16[128,512]{1,0:T(8,128)(2,1)}, u32[]{:S(2)}) %copy-start.3) | copy-done | bytes 131096
  5.7 0.0 copy-start.4
  5.7 0.9 %copy-done.4 = bf16[128,512]{1,0:T(8,128)(2,1)S(1)} copy-done((bf16[128,512]{1,0:T(8,128)(2,1)S(1)}, bf16[128,512]{1,0:T(8,128)(2,1)}, u32[]{:S(2)}) %copy-start.4) | copy-done | bytes 131096
  6.6 0.0 copy-start.5
  6.6 0.9 %copy-done.5 = bf16[1,128,512]{2,1,0:T(8,128)(2,1)S(1)} copy-done((bf16[1,128,512]{2,1,0:T(8,128)(2,1)S(1)}, bf16[1,128,512]{2,1,0:T(8,128)(2,1)}, u32[]{:S(2)}) %copy-start.5) | copy-done | bytes 131096
  7.5 46.8 %shard_map.127 = (bf16[128,512]{1,0:T(8,128)(2,1)S(1)}, bf16[128,512]{1,0:T(8,128)(2,1)S(1)}, bf16[128,512]{1,0:T(8,128)(2,1)S(1)}, bf16[128,512]{1,0:T(8,128)(2...) custom-call(bf16[128,512]{1,0:T(8,128)(2,1)S(1)} %bitcast.8, bf16[128,512]{1,0:T(8,128)(2,1)S(1)} %bitcast.9, ...), custom_call_target="tpu_custom_call" | custom-call | tf_op jit(solution)/shard_map/pallas_call | solution.py:389
  54.4 0.7 %copy.22 = bf16[1,128,512]{2,1,0:T(8,128)(2,1)} copy(bf16[1,128,512]{2,1,0:T(8,128)(2,1)S(1)} %bitcast.15) | data formatting | bytes 262144
  55.0 0.7 %copy.23 = bf16[1,128,512]{2,1,0:T(8,128)(2,1)} copy(bf16[1,128,512]{2,1,0:T(8,128)(2,1)S(1)} %bitcast.14) | data formatting | bytes 262144
  55.7 0.7 %copy.24 = bf16[1,128,512]{2,1,0:T(8,128)(2,1)} copy(bf16[1,128,512]{2,1,0:T(8,128)(2,1)S(1)} %bitcast.13) | data formatting | bytes 262144
  56.3 0.7 %copy.25 = bf16[1,128,512]{2,1,0:T(8,128)(2,1)} copy(bf16[1,128,512]{2,1,0:T(8,128)(2,1)S(1)} %bitcast.12) | data formatting | bytes 262144
  57.0 0.7 %copy.26 = f32[128,512]{1,0:T(8,128)} copy(f32[128,512]{1,0:T(8,128)S(1)} %get-tuple-element.28) | data formatting | bytes 524288
  57.7 0.7 %copy.27 = f32[128,512]{1,0:T(8,128)} copy(f32[128,512]{1,0:T(8,128)S(1)} %get-tuple-element.29) | data formatting | bytes 524288
Async XLA Ops:
  0.6 0.7 %copy-start.6 = (s32[16,3]{0,1:T(4,128)S(1)}, s32[16,3]{0,1:T(4,128)}, u32[]{:S(2)}) copy-start(s32[16,3]{0,1:T(4,128)} %param.14) | copy-start | bytes 580
  1.3 0.7 %copy-start.7 = (s32[16,3]{0,1:T(4,128)S(1)}, s32[16,3]{0,1:T(4,128)}, u32[]{:S(2)}) copy-start(s32[16,3]{0,1:T(4,128)} %param.15) | copy-start | bytes 580
  2.1 0.9 %copy-start = (bf16[1,128,512]{2,1,0:T(8,128)(2,1)S(1)}, bf16[1,128,512]{2,1,0:T(8,128)(2,1)}, u32[]{:S(2)}) copy-start(bf16[1,128,512]{2,1,0:T(8,128)(2,1)} %param.8) | copy-start | bytes 393220
  3.0 0.9 %copy-start.1 = (bf16[1,128,512]{2,1,0:T(8,128)(2,1)S(1)}, bf16[1,128,512]{2,1,0:T(8,128)(2,1)}, u32[]{:S(2)}) copy-start(bf16[1,128,512]{2,1,0:T(8,128)(2,1)} %param.9) | copy-start | bytes 393220
  3.9 0.9 %copy-start.2 = (bf16[1,128,512]{2,1,0:T(8,128)(2,1)S(1)}, bf16[1,128,512]{2,1,0:T(8,128)(2,1)}, u32[]{:S(2)}) copy-start(bf16[1,128,512]{2,1,0:T(8,128)(2,1)} %param.10) | copy-start | bytes 393220
  4.8 0.9 %copy-start.3 = (bf16[128,512]{1,0:T(8,128)(2,1)S(1)}, bf16[128,512]{1,0:T(8,128)(2,1)}, u32[]{:S(2)}) copy-start(bf16[128,512]{1,0:T(8,128)(2,1)} %gk_ref.1) | copy-start | bytes 393220
  5.7 0.9 %copy-start.4 = (bf16[128,512]{1,0:T(8,128)(2,1)S(1)}, bf16[128,512]{1,0:T(8,128)(2,1)}, u32[]{:S(2)}) copy-start(bf16[128,512]{1,0:T(8,128)(2,1)} %gv_ref.1) | copy-start | bytes 393220
  6.6 0.9 %copy-start.5 = (bf16[1,128,512]{2,1,0:T(8,128)(2,1)S(1)}, bf16[1,128,512]{2,1,0:T(8,128)(2,1)}, u32[]{:S(2)}) copy-start(bf16[1,128,512]{2,1,0:T(8,128)(2,1)} %param.13) | copy-start | bytes 393220

commit v2 on v1

--- a/solution.py
+++ b/solution.py
@@ -12,6 +12,7 @@
 BLOCK = 64
 R = 3
 LANES = 128
+VMEM_BYTES = 63 * 1024 * 1024
 MASKED = -1e30
 MESH = pl.DeviceIdType.MESH
 NT = (((1,), (1,)), ((), ()))
@@ -32,9 +33,20 @@
 
 
 def kernel(
-    shards, stages, q_ref, k_ref, v_ref, gk_ref, gv_ref, u_ref, ps_ref, pb_ref,
-    att_ref, dq_ref, dk_ref, dv_ref, dgk_ref, dgv_ref,
-    kv, bias, terms, back, own, *rest,
+    shards, stages, q_hbm, k_hbm, v_hbm, gk_hbm, gv_hbm, u_hbm, ps_hbm, pb_hbm,
+    *refs,
+):
+    outs_hbm, (att_ref, dq_ref, dk_ref, dv_ref, dgk_ref, dgv_ref) = refs[:6], refs[6:12]
+    run(
+        shards, stages, q_hbm, k_hbm, v_hbm, gk_hbm, gv_hbm, u_hbm, ps_hbm, pb_hbm, outs_hbm,
+        att_ref, dq_ref, dk_ref, dv_ref, dgk_ref, dgv_ref, *refs[12:],
+    )
+
+
+def run(
+    shards, stages, q_hbm, k_hbm, v_hbm, gk_hbm, gv_hbm, u_hbm, ps_hbm, pb_hbm, outs_hbm,
+    att_ref, dq_ref, dk_ref, dv_ref, dgk_ref, dgv_ref, out_sem,
+    q_ref, u_ref, ps_ref, pb_ref, in_sem, own_sem, kv, bias, terms, back, own, *rest,
 ):
     count = len(stages)
     accs, recvs = rest[:count], rest[count : 2 * count]
@@ -44,11 +56,11 @@
     rs_send, rs_recv = sems[:count], sems[count : 2 * count]
     ag_send, ag_recv = sems[2 * count : 3 * count], sems[3 * count :]
 
-    rows, width = q_ref.shape
+    rows, width = q_hbm.shape
     blocks = rows // BLOCK
     chunks = width // LANES
     bits = shards.bit_length() - 1
-    globals_ = gk_ref.shape[0]
+    globals_ = gk_hbm.shape[0]
     edge_at = rows * (1 + bits)
     glob_at = edge_at + BLOCK
     total = kv.shape[2]
@@ -79,10 +91,30 @@
         def _():
             greet("ctx", edge_peer)
 
+    own_copies, in_copies = [], []
     for c in range(chunks):
-        lanes = slice(c * LANES, (c + 1) * LANES)
-        kv[c, 0, 0:rows] = k_ref[:, lanes]
-        kv[c, 1, 0:rows] = v_ref[:, lanes]
+        lanes = pl.ds(c * LANES, LANES)
+        for which, (part, shared) in enumerate(((k_hbm, gk_hbm), (v_hbm, gv_hbm))):
+            own_copies.append(
+                pltpu.make_async_copy(
+                    part.at[:, lanes], kv.at[c, which, pl.ds(0, rows)], own_sem.at[0, c, which]
+                )
+            )
+            in_copies.append(
+                pltpu.make_async_copy(
+                    shared.at[:, lanes],
+                    kv.at[c, which, pl.ds(glob_at, globals_)],
+                    own_sem.at[1, c, which],
+                )
+            )
+    for i, (src, dst) in enumerate(
+        ((ps_hbm, ps_ref), (pb_hbm, pb_ref), (q_hbm, q_ref), (u_hbm, u_ref))
+    ):
+        in_copies.append(pltpu.make_async_copy(src, dst, in_sem.at[i]))
+    for copy in own_copies + in_copies:
+        copy.start()
+    for copy in own_copies:
+        copy.wait()
 
     pl.semaphore_wait(barrier, greeted + jnp.where(has_edge, 1, 0) if apart else greeted)
 
@@ -127,10 +159,9 @@
         def _():
             kv_edge(c).start()
 
+    for copy in in_copies:
+        copy.wait()
     for c in range(chunks):
-        lanes = slice(c * LANES, (c + 1) * LANES)
-        kv[c, 0, glob_at : glob_at + globals_] = gk_ref[:, lanes]
-        kv[c, 1, glob_at : glob_at + globals_] = gv_ref[:, lanes]
         if total > glob_at + globals_:
             kv[c, :, glob_at + globals_ :] = jnp.zeros(
                 (2, total - glob_at - globals_, LANES), kv.dtype
@@ -147,7 +178,7 @@
     query_block = lax.rem(lax.div(lax.broadcasted_iota(jnp.int32, (8, pair), 1), BLOCK), blocks)
     first_block = me * blocks
     listed = [
-        [(ps_ref[first_block + n, r], pb_ref[first_block + n, r]) for r in range(R)]
+        [(ps_ref[r, first_block + n], pb_ref[r, first_block + n]) for r in range(R)]
         for n in range(blocks)
     ]
 
@@ -200,6 +231,30 @@
 
     NN = (((1,), (0,)), ((), ()))
 
+    def by_query(x):
+        return jnp.concatenate([x[:HEAD_DIM, :rows], x[HEAD_DIM:, rows:]], axis=0).T
+
+    def digit_of(i):
+        axis, stride, radix, _ = stages[i]
+        return lax.rem(lax.div(spot[axis], stride), radix)
+
+    def peer_of(i, k):
+        axis, stride, radix, _ = stages[i]
+        digit = digit_of(i)
+        other = lax.rem(digit + k, radix)
+        return other, {axis: spot[axis] + (other - digit) * stride}
+
+    def scatter_copy(i, k):
+        held = stages[i][3]
+        other, device = peer_of(i, k)
+        at = other * held if accs[i].shape[0] != held else 0
+        return pltpu.make_async_remote_copy(
+            src_ref=accs[i].at[pl.ds(pl.multiple_of(at, 16), held)],
+            dst_ref=recvs[i].at[k - 1],
+            send_sem=rs_send[i].at[k - 1], recv_sem=rs_recv[i].at[k - 1],
+            device_id=device, device_id_type=MESH,
+        )
+
     def step(c, carry):
         lanes = pl.ds(pl.multiple_of(c * LANES, LANES), LANES)
         queries = (both_heads(q_ref[:, lanes]) * scaling).astype(jnp.bfloat16)
@@ -227,6 +282,16 @@
             accs[0][
                 pl.ds(pl.multiple_of((c * 2 + which) * globals_, globals_), globals_)
             ] = made[glob_at : glob_at + globals_].astype(jnp.bfloat16)
+        for k in range(1, stages[0][2]):
+            held = stages[0][3]
+            ready = lax.div((peer_of(0, k)[0] + 1) * held - 1, 2 * globals_)
+            if accs[0].shape[0] == held:
+                ready = chunks - 1
+
+            @pl.when(c == ready)
+            def _(k=k):
+                scatter_copy(0, k).start()
+
         for b in order:
             term_copy(c, b).start()
 
@@ -234,38 +299,19 @@
         def _():
             term_edge(c).start()
 
-        attention = dot(low, values, TN)
-        att_ref[:, lanes] = jnp.where(low_head, attention[:rows], attention[rows:]).astype(
-            jnp.bfloat16
-        )
-        dqueries = dot(dscores, keys, TN)
-        dq_ref[:, lanes] = (
-            jnp.where(low_head, dqueries[:rows], dqueries[rows:]) * scaling
-        ).astype(jnp.bfloat16)
+        att_ref[:, lanes] = by_query(dot(values, low, TN)).astype(jnp.bfloat16)
+        dq_ref[:, lanes] = (by_query(dot(keys, dscores, TN)) * scaling).astype(jnp.bfloat16)
         return carry
 
     lax.fori_loop(0, chunks, step, 0)
-
-    def digit_of(i):
-        axis, stride, radix, _ = stages[i]
-        return lax.rem(lax.div(spot[axis], stride), radix)
-
-    def peer_of(i, k):
-        axis, stride, radix, _ = stages[i]
-        digit = digit_of(i)
-        other = lax.rem(digit + k, radix)
-        return other, {axis: spot[axis] + (other - digit) * stride}
-
-    def scatter_copy(i, k):
-        held = stages[i][3]
-        other, device = peer_of(i, k)
-        at = other * held if accs[i].shape[0] != held else 0
-        return pltpu.make_async_remote_copy(
-            src_ref=accs[i].at[pl.ds(pl.multiple_of(at, 16), held)],
-            dst_ref=recvs[i].at[k - 1],
-            send_sem=rs_send[i].at[k - 1], recv_sem=rs_recv[i].at[k - 1],
-            device_id=device, device_id_type=MESH,
-        )
+    out_copies = [
+        pltpu.make_async_copy(ref, out, out_sem.at[i])
+        for i, (ref, out) in enumerate(
+            zip((att_ref, dq_ref, dk_ref, dv_ref, dgk_ref, dgv_ref), outs_hbm)
+        )
+    ]
+    out_copies[0].start()
+    out_copies[1].start()
 
     starts = []
     start = 0
@@ -331,7 +377,8 @@
             out[:, lanes] = summed.astype(jnp.bfloat16)
 
     for i in range(count):
-        scatter_start(i)
+        if i:
+            scatter_start(i)
         scatter_end(i)
     split = [i for i in range(count) if accs[i].shape[0] != stages[i][3]]
     todo = list(range(chunks))
@@ -345,8 +392,12 @@
         for which, out in enumerate((dgk_ref, dgv_ref)):
             at = (c * 2 + which) * globals_
             out[:, lanes] = final[at : at + globals_].astype(jnp.float32)
+    out_copies[4].start()
+    out_copies[5].start()
     for c in todo:
         collect(c)
+    out_copies[2].start()
+    out_copies[3].start()
 
     for c in range(chunks):
         for b in order:
@@ -363,6 +414,20 @@
             scatter_copy(i, k).wait_send()
             if i in split:
                 gather_copy(i, k, starts[i]).wait_send()
+
+    for copy in out_copies:
+        copy.wait()
+
+
+def write_out(*refs):
+    count = len(refs) // 2
+    copies = [
+        pltpu.make_async_copy(refs[i], refs[count + i], refs[-1].at[i]) for i in range(count)
+    ]
+    for copy in copies:
+        copy.start()
+    for copy in copies:
+        copy.wait()
 
 
 def body(shards, replicas, queries, keys, values, global_keys, global_values, upstream, ps, pb):
@@ -382,17 +447,24 @@
         recvs.append(pltpu.VMEM((radix - 1, after, LANES), low))
         sems.append(pltpu.SemaphoreType.DMA((radix - 1,)))
         held = after
-    vmem = pl.BlockSpec(memory_space=pltpu.VMEM)
-    smem = pl.BlockSpec(memory_space=pltpu.SMEM)
+    hbm = pl.BlockSpec(memory_space=pltpu.HBM)
     dma = pltpu.SemaphoreType.DMA((chunks, bits + 1))
     remote = rows * bits + BLOCK
+    results = [((rows, width), low)] * 4 + [((globals_, width), jnp.float32)] * 2
     outs = pl.pallas_call(
         functools.partial(kernel, shards, stages),
-        out_shape=[jax.ShapeDtypeStruct((rows, width), low)] * 4
-        + [jax.ShapeDtypeStruct((globals_, width), jnp.float32)] * 2,
-        in_specs=[vmem] * 6 + [smem] * 2,
-        out_specs=[vmem] * 6,
+        out_shape=[jax.ShapeDtypeStruct(*x) for x in results],
+        in_specs=[hbm] * 8,
+        out_specs=[hbm] * 6,
         scratch_shapes=[
+            *[pltpu.VMEM(*x) for x in results],
+            pltpu.SemaphoreType.DMA((6,)),
+            pltpu.VMEM((rows, width), low),
+            pltpu.VMEM((rows, width), low),
+            pltpu.SMEM(ps.T.shape, jnp.int32),
+            pltpu.SMEM(pb.T.shape, jnp.int32),
+            pltpu.SemaphoreType.DMA((4,)),
+            pltpu.SemaphoreType.DMA((2, chunks, 2)),
             pltpu.VMEM((chunks, 2, total, LANES), low),
             pltpu.VMEM((total, 2 * rows), jnp.float32),
             pltpu.VMEM((chunks, 2, remote, LANES), low),
@@ -405,9 +477,17 @@
             *sems, *sems, *sems, *sems,
         ],
         compiler_params=pltpu.CompilerParams(
-            collective_id=0, has_side_effects=True, vmem_limit_bytes=40 * 1024 * 1024
+            collective_id=0, has_side_effects=True, vmem_limit_bytes=VMEM_BYTES
         ),
-    )(queries[0], keys[0], values[0], global_keys, global_values, upstream[0], ps, pb)
+    )(queries[0], keys[0], values[0], global_keys, global_values, upstream[0], ps.T, pb.T)
+    outs = pl.pallas_call(
+        write_out,
+        out_shape=[jax.ShapeDtypeStruct(x.shape, x.dtype) for x in outs],
+        in_specs=[hbm] * 6,
+        out_specs=[hbm] * 6,
+        scratch_shapes=[pltpu.SemaphoreType.DMA((6,))],
+        compiler_params=pltpu.CompilerParams(vmem_limit_bytes=VMEM_BYTES),
+    )(*outs)
     return (outs[0][None], outs[1][None], outs[2][None], outs[3][None], outs[4], outs[5])
 
 

time: 58.7 us -> 80.7 us (1.37)
  Pallas kernels: 46.8 us -> 79.9 us
  local copies, waits for them, and re-layouts: 10.9 us -> 0 us
    pallas_call x0 -> x1, Pallas kernels: none -> 32.9 us  [body(): pl.pallas_call(write_out, out_shape=[jax.ShapeDtypeStruct(x.shape, x.dtyp...]
    unnamed x24 -> x0, local copies, waits for them, and re-layouts: 10.9 us -> none
where the time goes in v2:
time: 80.7 us; the launch traced here: 80.6 us
  Pallas kernels  79.9 us (99%)
    pallas_call x1, Pallas kernels, body(): pl.pallas_call(functools.partial(kernel, shards, stages), out_shape=[jax....  47 us
    pallas_call x1, Pallas kernels, body(): pl.pallas_call(write_out, out_shape=[jax.ShapeDtypeStruct(x.shape, x.dtyp...  32.9 us

profile of v2, /device:TPU:1, one launch (start us, length us, event | category | flops | bytes accessed | tf_op | source)
XLA Modules:
  0.0 80.6 jit_solution(14520682945069312738)
XLA Ops:
  0.6 47.0 %shard_map.127 = (bf16[128,512]{1,0:T(8,128)(2,1)}, bf16[128,512]{1,0:T(8,128)(2,1)}, bf16[128,512]{1,0:T(8,128)(2,1)}, bf16[128,512]{1,0:T(8,128)(2,1)}, f32[128,512]{1,0:T(8,128)}, /*index=5*/f32[128,512]{1,0:T(8,128)}) custom-call(bf16[128,512]{1,0:T(8,128)(2,1)} %bitcast.10, bf16[128,512]{1,0:T(8,128)(2,1)} %bitcast.11, bf16[128,512]{1,0:T(8,128)(2,1)} %bitcast.12, ...), custom_call_target="tpu_custom_call" | custom-call | tf_op jit(solution)/shard_map/pallas_call | solution.py:454
  47.6 32.9 %shard_map.128 = (bf16[128,512]{1,0:T(8,128)(2,1)}, bf16[128,512]{1,0:T(8,128)(2,1)}, bf16[128,512]{1,0:T(8,128)(2,1)}, bf16[128,512]{1,0:T(8,128)(2,1)}, f32[128,512]{1,0:T(8,128)}, /*index=5*/f32[128,512]{1,0:T(8,128)}) custom-call(bf16[128,512]{1,0:T(8,128)(2,1)} %get-tuple-element.18.refs_0_, bf16[128,512]{1,0:T(8,128)(2,1)} %get-tuple-element.19.refs_1_, ...), custom_call_target="tpu_custom_call" | custom-call | tf_op jit(solution)/shard_map/pallas_call | solution.py:483

commit v3 on v2

--- a/solution.py
+++ b/solution.py
@@ -151,13 +151,26 @@
         )
 
     order = list(range(bits))[::-1]
-    for c in range(chunks):
+
+    def send_kv(c):
         for b in order:
             kv_copy(c, b).start()
 
         @pl.when(has_edge)
         def _():
             kv_edge(c).start()
+
+    def send_terms(c):
+        for b in order:
+            term_copy(c, b).start()
+
+        @pl.when(has_edge)
+        def _():
+            term_edge(c).start()
+
+    ahead = min(2, chunks)
+    for c in range(ahead):
+        send_kv(c)
 
     for copy in in_copies:
         copy.wait()
@@ -266,6 +279,10 @@
         def _():
             kv_edge(c).wait_recv()
 
+        @pl.when(c + ahead < chunks)
+        def _():
+            send_kv(c + ahead)
+
         keys = kv[c, 0]
         values = kv[c, 1]
         scores = dot(keys, queries, NT) + bias[...]
@@ -292,12 +309,9 @@
             def _(k=k):
                 scatter_copy(0, k).start()
 
-        for b in order:
-            term_copy(c, b).start()
-
-        @pl.when(has_edge)
-        def _():
-            term_edge(c).start()
+        @pl.when(c < chunks - 2)
+        def _():
+            send_terms(c)
 
         att_ref[:, lanes] = by_query(dot(values, low, TN)).astype(jnp.bfloat16)
         dq_ref[:, lanes] = (by_query(dot(keys, dscores, TN)) * scaling).astype(jnp.bfloat16)
@@ -379,11 +393,15 @@
     for i in range(count):
         if i:
             scatter_start(i)
+        if i == count - 1 and chunks > 1:
+            send_terms(chunks - 2)
         scatter_end(i)
     split = [i for i in range(count) if accs[i].shape[0] != stages[i][3]]
     todo = list(range(chunks))
     for i in split[::-1]:
         gather_start(i)
+        if i == split[-1]:
+            send_terms(chunks - 1)
         if todo:
             collect(todo.pop(0))
         gather_end(i)
@@ -420,13 +438,21 @@
 
 
 def write_out(*refs):
-    count = len(refs) // 2
-    copies = [
-        pltpu.make_async_copy(refs[i], refs[count + i], refs[-1].at[i]) for i in range(count)
+    count = len(refs) // 3
+    sem = refs[-1]
+    loads = [
+        pltpu.make_async_copy(refs[i], refs[2 * count + i], sem.at[0, i]) for i in range(count)
     ]
-    for copy in copies:
+    stores = [
+        pltpu.make_async_copy(refs[2 * count + i], refs[count + i], sem.at[1, i])
+        for i in range(count)
+    ]
+    for copy in loads:
         copy.start()
-    for copy in copies:
+    for load, store in zip(loads, stores):
+        load.wait()
+        store.start()
+    for copy in stores:
         copy.wait()
 
 
@@ -485,7 +511,10 @@
         out_shape=[jax.ShapeDtypeStruct(x.shape, x.dtype) for x in outs],
         in_specs=[hbm] * 6,
         out_specs=[hbm] * 6,
-        scratch_shapes=[pltpu.SemaphoreType.DMA((6,))],
+        scratch_shapes=[
+            *[pltpu.VMEM(*x) for x in results],
+            pltpu.SemaphoreType.DMA((2, 6)),
+        ],
         compiler_params=pltpu.CompilerParams(vmem_limit_bytes=VMEM_BYTES),
     )(*outs)
     return (outs[0][None], outs[1][None], outs[2][None], outs[3][None], outs[4], outs[5])

time: 80.7 us -> 46.5 us (0.58)
  Pallas kernels: 79.9 us -> 45.7 us
    pallas_call x1, Pallas kernels: 32.9 us -> 2.11 us  [body(): pl.pallas_call(write_out, out_shape=[jax.ShapeDtypeStruct(x.shape, x.dtyp...]
    pallas_call x1, Pallas kernels: 47 us -> 43.5 us  [body(): pl.pallas_call(functools.partial(kernel, shards, stages), out_shape=[jax....]
where the time goes in v3:
time: 46.5 us; the launch traced here: 46.3 us
  Pallas kernels  45.7 us (98%)
  between operations  0.64 us (1%)
    pallas_call x1, Pallas kernels, body(): pl.pallas_call(functools.partial(kernel, shards, stages), out_shape=[jax....  43.5 us
    pallas_call x1, Pallas kernels, body(): pl.pallas_call(write_out, out_shape=[jax.ShapeDtypeStruct(x.shape, x.dtyp...  2.11 us

profile of v3, /device:TPU:1, one launch (start us, length us, event | category | flops | bytes accessed | tf_op | source)
XLA Modules:
  0.0 46.3 jit_solution(14842824105964062387)
XLA Ops:
  0.6 43.5 %shard_map.127 = (bf16[128,512]{1,0:T(8,128)(2,1)}, bf16[128,512]{1,0:T(8,128)(2,1)}, bf16[128,512]{1,0:T(8,128)(2,1)}, bf16[128,512]{1,0:T(8,128)(2,1)}, f32[128,512]{1,0:T(8,128)}, /*index=5*/f32[128,512]{1,0:T(8,128)}) custom-call(bf16[128,512]{1,0:T(8,128)(2,1)} %bitcast.10, bf16[128,512]{1,0:T(8,128)(2,1)} %bitcast.11, bf16[128,512]{1,0:T(8,128)(2,1)} %bitcast.12, ...), custom_call_target="tpu_custom_call" | custom-call | tf_op jit(solution)/shard_map/pallas_call | solution.py:480
  44.2 2.1 %shard_map.128 = (bf16[128,512]{1,0:T(8,128)(2,1)}, bf16[128,512]{1,0:T(8,128)(2,1)}, bf16[128,512]{1,0:T(8,128)(2,1)}, bf16[128,512]{1,0:T(8,128)(2,1)}, f32[128,512]{1,0:T(8,128)}, /*index=5*/f32[128,512]{1,0:T(8,128)}) custom-call(bf16[128,512]{1,0:T(8,128)(2,1)} %get-tuple-element.18.refs_0_, bf16[128,512]{1,0:T(8,128)(2,1)} %get-tuple-element.19.refs_1_, ...), custom_call_target="tpu_custom_call" | custom-call | tf_op jit(solution)/shard_map/pallas_call | solution.py:509

commit v4 on v3

--- a/solution.py
+++ b/solution.py
@@ -169,8 +169,7 @@
             term_edge(c).start()
 
     ahead = min(2, chunks)
-    for c in range(ahead):
-        send_kv(c)
+    send_kv(0)
 
     for copy in in_copies:
         copy.wait()
@@ -273,7 +272,12 @@
         queries = (both_heads(q_ref[:, lanes]) * scaling).astype(jnp.bfloat16)
         grads = both_heads(u_ref[:, lanes]).astype(jnp.bfloat16)
         for b in order:
-            kv_copy(c, b).wait_recv()
+            if b:
+                kv_copy(c, b).wait_recv()
+
+        @pl.when(c > 0)
+        def _():
+            kv_copy(c, 0).wait_recv()
 
         @pl.when(has_edge)
         def _():
@@ -292,13 +296,11 @@
         dprobs = dot(values, grads, NT)
         inner = jnp.sum(probs * dprobs, axis=0, keepdims=True)
         dscores = (probs * (dprobs - inner)).astype(jnp.bfloat16)
-        for which, (left, right) in enumerate(((dscores, queries), (low, grads))):
-            made = dot(left, right, NN)
-            own[c, which] = made[0:rows]
-            terms[c, which] = made[rows:glob_at].astype(jnp.bfloat16)
+        pairs = ((dscores, queries), (low, grads))
+        for which, (left, right) in enumerate(pairs):
             accs[0][
                 pl.ds(pl.multiple_of((c * 2 + which) * globals_, globals_), globals_)
-            ] = made[glob_at : glob_at + globals_].astype(jnp.bfloat16)
+            ] = dot(left[glob_at : glob_at + globals_], right, NN).astype(jnp.bfloat16)
         for k in range(1, stages[0][2]):
             held = stages[0][3]
             ready = lax.div((peer_of(0, k)[0] + 1) * held - 1, 2 * globals_)
@@ -309,7 +311,12 @@
             def _(k=k):
                 scatter_copy(0, k).start()
 
-        @pl.when(c < chunks - 2)
+        for which, (left, right) in enumerate(pairs):
+            made = dot(left[:glob_at], right, NN)
+            own[c, which] = made[0:rows]
+            terms[c, which] = made[rows:].astype(jnp.bfloat16)
+
+        @pl.when(c < chunks - 1)
         def _():
             send_terms(c)
 
@@ -317,6 +324,9 @@
         dq_ref[:, lanes] = (by_query(dot(keys, dscores, TN)) * scaling).astype(jnp.bfloat16)
         return carry
 
+    kv_copy(0, 0).wait_recv()
+    for c in range(1, ahead):
+        send_kv(c)
     lax.fori_loop(0, chunks, step, 0)
     out_copies = [
         pltpu.make_async_copy(ref, out, out_sem.at[i])
@@ -390,19 +400,19 @@
             summed = summed + jnp.where(at_edge, edge, 0.0)
             out[:, lanes] = summed.astype(jnp.bfloat16)
 
+    todo = list(range(chunks))
     for i in range(count):
         if i:
             scatter_start(i)
-        if i == count - 1 and chunks > 1:
-            send_terms(chunks - 2)
+        if i and i == count - 1 and todo:
+            collect(todo.pop(0))
         scatter_end(i)
     split = [i for i in range(count) if accs[i].shape[0] != stages[i][3]]
-    todo = list(range(chunks))
     for i in split[::-1]:
         gather_start(i)
         if i == split[-1]:
             send_terms(chunks - 1)
-        if todo:
+        if len(todo) > 1:
             collect(todo.pop(0))
         gather_end(i)
     for c in range(chunks):

time: 46.5 us -> 46.7 us (level)
  no operation moved by 1% of the time
where the time goes in v4:
time: 46.7 us; the launch traced here: 46.5 us
  Pallas kernels  45.9 us (98%)
  between operations  0.64 us (1%)
    pallas_call x1, Pallas kernels, body(): pl.pallas_call(functools.partial(kernel, shards, stages), out_shape=[jax....  43.8 us
    pallas_call x1, Pallas kernels, body(): pl.pallas_call(write_out, out_shape=[jax.ShapeDtypeStruct(x.shape, x.dtyp...  2.11 us

profile of v4, /device:TPU:1, one launch (start us, length us, event | category | flops | bytes accessed | tf_op | source)
XLA Modules:
  0.0 46.5 jit_solution(3124056484304583566)
XLA Ops:
  0.6 43.8 %shard_map.127 = (bf16[128,512]{1,0:T(8,128)(2,1)}, bf16[128,512]{1,0:T(8,128)(2,1)}, bf16[128,512]{1,0:T(8,128)(2,1)}, bf16[128,512]{1,0:T(8,128)(2,1)}, f32[128,512]{1,0:T(8,128)}, /*index=5*/f32[128,512]{1,0:T(8,128)}) custom-call(bf16[128,512]{1,0:T(8,128)(2,1)} %bitcast.10, bf16[128,512]{1,0:T(8,128)(2,1)} %bitcast.11, bf16[128,512]{1,0:T(8,128)(2,1)} %bitcast.12, ...), custom_call_target="tpu_custom_call" | custom-call | tf_op jit(solution)/shard_map/pallas_call | solution.py:490
  44.4 2.1 %shard_map.128 = (bf16[128,512]{1,0:T(8,128)(2,1)}, bf16[128,512]{1,0:T(8,128)(2,1)}, bf16[128,512]{1,0:T(8,128)(2,1)}, bf16[128,512]{1,0:T(8,128)(2,1)}, f32[128,512]{1,0:T(8,128)}, /*index=5*/f32[128,512]{1,0:T(8,128)}) custom-call(bf16[128,512]{1,0:T(8,128)(2,1)} %get-tuple-element.18.refs_0_, bf16[128,512]{1,0:T(8,128)(2,1)} %get-tuple-element.19.refs_1_, ...), custom_call_target="tpu_custom_call" | custom-call | tf_op jit(solution)/shard_map/pallas_call | solution.py:519

commit v5 on v4

--- a/solution.py
+++ b/solution.py
@@ -169,7 +169,8 @@
             term_edge(c).start()
 
     ahead = min(2, chunks)
-    send_kv(0)
+    for c in range(ahead):
+        send_kv(c)
 
     for copy in in_copies:
         copy.wait()
@@ -272,12 +273,7 @@
         queries = (both_heads(q_ref[:, lanes]) * scaling).astype(jnp.bfloat16)
         grads = both_heads(u_ref[:, lanes]).astype(jnp.bfloat16)
         for b in order:
-            if b:
-                kv_copy(c, b).wait_recv()
-
-        @pl.when(c > 0)
-        def _():
-            kv_copy(c, 0).wait_recv()
+            kv_copy(c, b).wait_recv()
 
         @pl.when(has_edge)
         def _():
@@ -286,6 +282,11 @@
         @pl.when(c + ahead < chunks)
         def _():
             send_kv(c + ahead)
+
+        @pl.when(c == chunks - 1)
+        def _():
+            for done in range(chunks - 2):
+                send_terms(done)
 
         keys = kv[c, 0]
         values = kv[c, 1]
@@ -316,17 +317,10 @@
             own[c, which] = made[0:rows]
             terms[c, which] = made[rows:].astype(jnp.bfloat16)
 
-        @pl.when(c < chunks - 1)
-        def _():
-            send_terms(c)
-
         att_ref[:, lanes] = by_query(dot(values, low, TN)).astype(jnp.bfloat16)
         dq_ref[:, lanes] = (by_query(dot(keys, dscores, TN)) * scaling).astype(jnp.bfloat16)
         return carry
 
-    kv_copy(0, 0).wait_recv()
-    for c in range(1, ahead):
-        send_kv(c)
     lax.fori_loop(0, chunks, step, 0)
     out_copies = [
         pltpu.make_async_copy(ref, out, out_sem.at[i])
@@ -404,8 +398,8 @@
     for i in range(count):
         if i:
             scatter_start(i)
-        if i and i == count - 1 and todo:
-            collect(todo.pop(0))
+        if i == count - 1 and chunks > 1:
+            send_terms(chunks - 2)
         scatter_end(i)
     split = [i for i in range(count) if accs[i].shape[0] != stages[i][3]]
     for i in split[::-1]:

time: 46.7 us -> 45.7 us (0.979)
  Pallas kernels: 45.9 us -> 44.9 us
    pallas_call x1, Pallas kernels: 43.8 us -> 42.8 us  [body(): pl.pallas_call(functools.partial(kernel, shards, stages), out_shape=[jax....]
where the time goes in v5:
time: 45.7 us; the launch traced here: 45.6 us
  Pallas kernels  44.9 us (98%)
  between operations  0.64 us (1%)
    pallas_call x1, Pallas kernels, body(): pl.pallas_call(functools.partial(kernel, shards, stages), out_shape=[jax....  42.8 us
    pallas_call x1, Pallas kernels, body(): pl.pallas_call(write_out, out_shape=[jax.ShapeDtypeStruct(x.shape, x.dtyp...  2.11 us

profile of v5, /device:TPU:1, one launch (start us, length us, event | category | flops | bytes accessed | tf_op | source)
XLA Modules:
  0.0 45.6 jit_solution(15489646679246479663)
XLA Ops:
  0.6 42.8 %shard_map.127 = (bf16[128,512]{1,0:T(8,128)(2,1)}, bf16[128,512]{1,0:T(8,128)(2,1)}, bf16[128,512]{1,0:T(8,128)(2,1)}, bf16[128,512]{1,0:T(8,128)(2,1)}, f32[128,512]{1,0:T(8,128)}, /*index=5*/f32[128,512]{1,0:T(8,128)}) custom-call(bf16[128,512]{1,0:T(8,128)(2,1)} %bitcast.10, bf16[128,512]{1,0:T(8,128)(2,1)} %bitcast.11, bf16[128,512]{1,0:T(8,128)(2,1)} %bitcast.12, ...), custom_call_target="tpu_custom_call" | custom-call | tf_op jit(solution)/shard_map/pallas_call | solution.py:484
  43.5 2.1 %shard_map.128 = (bf16[128,512]{1,0:T(8,128)(2,1)}, bf16[128,512]{1,0:T(8,128)(2,1)}, bf16[128,512]{1,0:T(8,128)(2,1)}, bf16[128,512]{1,0:T(8,128)(2,1)}, f32[128,512]{1,0:T(8,128)}, /*index=5*/f32[128,512]{1,0:T(8,128)}) custom-call(bf16[128,512]{1,0:T(8,128)(2,1)} %get-tuple-element.18.refs_0_, bf16[128,512]{1,0:T(8,128)(2,1)} %get-tuple-element.19.refs_1_, ...), custom_call_target="tpu_custom_call" | custom-call | tf_op jit(solution)/shard_map/pallas_call | solution.py:513

commit v6 on v5

--- a/solution.py
+++ b/solution.py
@@ -46,7 +46,7 @@
 def run(
     shards, stages, q_hbm, k_hbm, v_hbm, gk_hbm, gv_hbm, u_hbm, ps_hbm, pb_hbm, outs_hbm,
     att_ref, dq_ref, dk_ref, dv_ref, dgk_ref, dgv_ref, out_sem,
-    q_ref, u_ref, ps_ref, pb_ref, in_sem, own_sem, kv, bias, terms, back, own, *rest,
+    q_ref, u_ref, ps_ref, pb_ref, in_sem, own_sem, weight_s, dprob_s, low_s, dscore_s, kv, bias, terms, back, own, *rest,
 ):
     count = len(stages)
     accs, recvs = rest[:count], rest[count : 2 * count]
@@ -63,7 +63,7 @@
     globals_ = gk_hbm.shape[0]
     edge_at = rows * (1 + bits)
     glob_at = edge_at + BLOCK
-    total = kv.shape[2]
+    tiles = [(rows * i, rows) for i in range(1 + bits)] + [(edge_at, BLOCK), (glob_at, globals_)]
     me = lax.axis_index("ctx")
     spot = {"ctx": me, "dp": lax.axis_index("dp")}
     odd = lax.rem(me, 2)
@@ -174,11 +174,6 @@
 
     for copy in in_copies:
         copy.wait()
-    for c in range(chunks):
-        if total > glob_at + globals_:
-            kv[c, :, glob_at + globals_ :] = jnp.zeros(
-                (2, total - glob_at - globals_, LANES), kv.dtype
-            )
 
     @pl.when(jnp.logical_not(has_edge))
     def _():
@@ -226,8 +221,6 @@
     put_bias(edge_at, edge_counts)
     for at in range(glob_at, glob_at + globals_, BLOCK):
         put_bias(at, [jnp.int32(1)] * blocks)
-    if total > glob_at + globals_:
-        bias[glob_at + globals_ :] = jnp.full((total - glob_at - globals_, pair), MASKED)
 
     low_head = lax.broadcasted_iota(jnp.int32, (rows, LANES), 1) < HEAD_DIM
     scaling = 1.0 / math.sqrt(HEAD_DIM)
@@ -288,20 +281,38 @@
             for done in range(chunks - 2):
                 send_terms(done)
 
-        keys = kv[c, 0]
-        values = kv[c, 1]
-        scores = dot(keys, queries, NT) + bias[...]
-        weights = jnp.exp(scores - jnp.max(scores, axis=0, keepdims=True))
-        probs = weights * (1.0 / jnp.sum(weights, axis=0, keepdims=True))
-        low = probs.astype(jnp.bfloat16)
-        dprobs = dot(values, grads, NT)
-        inner = jnp.sum(probs * dprobs, axis=0, keepdims=True)
-        dscores = (probs * (dprobs - inner)).astype(jnp.bfloat16)
-        pairs = ((dscores, queries), (low, grads))
-        for which, (left, right) in enumerate(pairs):
+        top = None
+        for at, size in tiles:
+            rows_at = slice(at, at + size)
+            scores = dot(kv[c, 0, rows_at], queries, NT) + bias[rows_at]
+            weight_s[rows_at] = scores
+            part = jnp.max(scores, axis=0, keepdims=True)
+            top = part if top is None else jnp.maximum(top, part)
+        norm = mixed = jnp.zeros((1, pair), jnp.float32)
+        for at, size in tiles:
+            rows_at = slice(at, at + size)
+            weights = jnp.exp(weight_s[rows_at] - top)
+            dprobs = dot(kv[c, 1, rows_at], grads, NT)
+            weight_s[rows_at] = weights
+            dprob_s[rows_at] = dprobs
+            norm = norm + jnp.sum(weights, axis=0, keepdims=True)
+            mixed = mixed + jnp.sum(weights * dprobs, axis=0, keepdims=True)
+        inverse = 1.0 / norm
+        inner = mixed * inverse
+
+        def products(at, size):
+            rows_at = slice(at, at + size)
+            probs = weight_s[rows_at] * inverse
+            low = probs.astype(jnp.bfloat16)
+            dscores = (probs * (dprob_s[rows_at] - inner)).astype(jnp.bfloat16)
+            low_s[rows_at] = low
+            dscore_s[rows_at] = dscores
+            return dot(dscores, queries, NN), dot(low, grads, NN)
+
+        for which, made in enumerate(products(*tiles[-1])):
             accs[0][
                 pl.ds(pl.multiple_of((c * 2 + which) * globals_, globals_), globals_)
-            ] = dot(left[glob_at : glob_at + globals_], right, NN).astype(jnp.bfloat16)
+            ] = made.astype(jnp.bfloat16)
         for k in range(1, stages[0][2]):
             held = stages[0][3]
             ready = lax.div((peer_of(0, k)[0] + 1) * held - 1, 2 * globals_)
@@ -312,13 +323,15 @@
             def _(k=k):
                 scatter_copy(0, k).start()
 
-        for which, (left, right) in enumerate(pairs):
-            made = dot(left[:glob_at], right, NN)
-            own[c, which] = made[0:rows]
-            terms[c, which] = made[rows:].astype(jnp.bfloat16)
-
-        att_ref[:, lanes] = by_query(dot(values, low, TN)).astype(jnp.bfloat16)
-        dq_ref[:, lanes] = (by_query(dot(keys, dscores, TN)) * scaling).astype(jnp.bfloat16)
+        for at, size in tiles[1:-1]:
+            for which, made in enumerate(products(at, size)):
+                terms[c, which, at - rows : at - rows + size] = made.astype(jnp.bfloat16)
+        for which, made in enumerate(products(*tiles[0])):
+            own[c, which] = made
+        att_ref[:, lanes] = by_query(dot(kv[c, 1], low_s[...], TN)).astype(jnp.bfloat16)
+        dq_ref[:, lanes] = (by_query(dot(kv[c, 0], dscore_s[...], TN)) * scaling).astype(
+            jnp.bfloat16
+        )
         return carry
 
     lax.fori_loop(0, chunks, step, 0)
@@ -465,8 +478,7 @@
     globals_ = global_keys.shape[0]
     bits = shards.bit_length() - 1
     chunks = width // LANES
-    used = rows * (1 + bits) + BLOCK + globals_
-    total = -(-used // LANES) * LANES
+    total = rows * (1 + bits) + BLOCK + globals_
     gathered = 2 * chunks * globals_
     stages = reduce_stages((("dp", replicas), ("ctx", shards)), gathered)
     low = jnp.bfloat16
@@ -495,6 +507,7 @@
             pltpu.SMEM(pb.T.shape, jnp.int32),
             pltpu.SemaphoreType.DMA((4,)),
             pltpu.SemaphoreType.DMA((2, chunks, 2)),
+            *[pltpu.VMEM((total, 2 * rows), x) for x in (jnp.float32, jnp.float32, low, low)],
             pltpu.VMEM((chunks, 2, total, LANES), low),
             pltpu.VMEM((total, 2 * rows), jnp.float32),
             pltpu.VMEM((chunks, 2, remote, LANES), low),

time: 45.7 us -> 45.5 us (level)
  no operation moved by 1% of the time
where the time goes in v6:
time: 45.5 us; the launch traced here: 45.4 us
  Pallas kernels  44.7 us (98%)
  between operations  0.64 us (1%)
    pallas_call x1, Pallas kernels, body(): pl.pallas_call(functools.partial(kernel, shards, stages), out_shape=[jax....  42.6 us
    pallas_call x1, Pallas kernels, body(): pl.pallas_call(write_out, out_shape=[jax.ShapeDtypeStruct(x.shape, x.dtyp...  2.11 us

profile of v6, /device:TPU:1, one launch (start us, length us, event | category | flops | bytes accessed | tf_op | source)
XLA Modules:
  0.0 45.4 jit_solution(9327543383534522550)
XLA Ops:
  0.6 42.6 %shard_map.127 = (bf16[128,512]{1,0:T(8,128)(2,1)}, bf16[128,512]{1,0:T(8,128)(2,1)}, bf16[128,512]{1,0:T(8,128)(2,1)}, bf16[128,512]{1,0:T(8,128)(2,1)}, f32[128,512]{1,0:T(8,128)}, /*index=5*/f32[128,512]{1,0:T(8,128)}) custom-call(bf16[128,512]{1,0:T(8,128)(2,1)} %bitcast.10, bf16[128,512]{1,0:T(8,128)(2,1)} %bitcast.11, bf16[128,512]{1,0:T(8,128)(2,1)} %bitcast.12, ...), custom_call_target="tpu_custom_call" | custom-call | tf_op jit(solution)/shard_map/pallas_call | solution.py:496
  43.3 2.1 %shard_map.128 = (bf16[128,512]{1,0:T(8,128)(2,1)}, bf16[128,512]{1,0:T(8,128)(2,1)}, bf16[128,512]{1,0:T(8,128)(2,1)}, bf16[128,512]{1,0:T(8,128)(2,1)}, f32[128,512]{1,0:T(8,128)}, /*index=5*/f32[128,512]{1,0:T(8,128)}) custom-call(bf16[128,512]{1,0:T(8,128)(2,1)} %get-tuple-element.18.refs_0_, bf16[128,512]{1,0:T(8,128)(2,1)} %get-tuple-element.19.refs_1_, ...), custom_call_target="tpu_custom_call" | custom-call | tf_op jit(solution)/shard_map/pallas_call | solution.py:526

commit v7 on v6

--- a/solution.py
+++ b/solution.py
@@ -168,7 +168,7 @@
         def _():
             term_edge(c).start()
 
-    ahead = min(2, chunks)
+    ahead = min(3, chunks)
     for c in range(ahead):
         send_kv(c)
 
@@ -276,11 +276,6 @@
         def _():
             send_kv(c + ahead)
 
-        @pl.when(c == chunks - 1)
-        def _():
-            for done in range(chunks - 2):
-                send_terms(done)
-
         top = None
         for at, size in tiles:
             rows_at = slice(at, at + size)
@@ -326,6 +321,11 @@
         for at, size in tiles[1:-1]:
             for which, made in enumerate(products(at, size)):
                 terms[c, which, at - rows : at - rows + size] = made.astype(jnp.bfloat16)
+
+        @pl.when(c < chunks - 1)
+        def _():
+            send_terms(c)
+
         for which, made in enumerate(products(*tiles[0])):
             own[c, which] = made
         att_ref[:, lanes] = by_query(dot(kv[c, 1], low_s[...], TN)).astype(jnp.bfloat16)
@@ -411,8 +411,6 @@
     for i in range(count):
         if i:
             scatter_start(i)
-        if i == count - 1 and chunks > 1:
-            send_terms(chunks - 2)
         scatter_end(i)
     split = [i for i in range(count) if accs[i].shape[0] != stages[i][3]]
     for i in split[::-1]:

time: 45.5 us -> 46.5 us (1.022)
  Pallas kernels: 44.7 us -> 45.7 us
    pallas_call x1, Pallas kernels: 42.6 us -> 43.6 us  [body(): pl.pallas_call(functools.partial(kernel, shards, stages), out_shape=[jax....]
where the time goes in v7:
time: 46.5 us; the launch traced here: 46.4 us
  Pallas kernels  45.7 us (98%)
  between operations  0.64 us (1%)
    pallas_call x1, Pallas kernels, body(): pl.pallas_call(functools.partial(kernel, shards, stages), out_shape=[jax....  43.6 us
    pallas_call x1, Pallas kernels, body(): pl.pallas_call(write_out, out_shape=[jax.ShapeDtypeStruct(x.shape, x.dtyp...  2.11 us

profile of v7, /device:TPU:1, one launch (start us, length us, event | category | flops | bytes accessed | tf_op | source)
XLA Modules:
  0.0 46.4 jit_solution(13781866240891979721)
XLA Ops:
  0.6 43.6 %shard_map.127 = (bf16[128,512]{1,0:T(8,128)(2,1)}, bf16[128,512]{1,0:T(8,128)(2,1)}, bf16[128,512]{1,0:T(8,128)(2,1)}, bf16[128,512]{1,0:T(8,128)(2,1)}, f32[128,512]{1,0:T(8,128)}, /*index=5*/f32[128,512]{1,0:T(8,128)}) custom-call(bf16[128,512]{1,0:T(8,128)(2,1)} %bitcast.10, bf16[128,512]{1,0:T(8,128)(2,1)} %bitcast.11, bf16[128,512]{1,0:T(8,128)(2,1)} %bitcast.12, ...), custom_call_target="tpu_custom_call" | custom-call | tf_op jit(solution)/shard_map/pallas_call | solution.py:494
  44.3 2.1 %shard_map.128 = (bf16[128,512]{1,0:T(8,128)(2,1)}, bf16[128,512]{1,0:T(8,128)(2,1)}, bf16[128,512]{1,0:T(8,128)(2,1)}, bf16[128,512]{1,0:T(8,128)(2,1)}, f32[128,512]{1,0:T(8,128)}, /*index=5*/f32[128,512]{1,0:T(8,128)}) custom-call(bf16[128,512]{1,0:T(8,128)(2,1)} %get-tuple-element.18.refs_0_, bf16[128,512]{1,0:T(8,128)(2,1)} %get-tuple-element.19.refs_1_, ...), custom_call_target="tpu_custom_call" | custom-call | tf_op jit(solution)/shard_map/pallas_call | solution.py:524

commit v8 on v6

--- a/solution.py
+++ b/solution.py
@@ -24,7 +24,7 @@
     for axis, size in sizes:
         stride = 1
         while stride < size:
-            radix = min(8, size // stride)
+            radix = min(2 if axis == "ctx" and stride == 1 else 8, size // stride)
             if rows % (radix * 16) == 0:
                 rows //= radix
             stages.append((axis, stride, radix, rows))

time: 45.5 us -> 46.6 us (1.024)
  Pallas kernels: 44.7 us -> 45.8 us
    pallas_call x1, Pallas kernels: 42.6 us -> 43.7 us  [body(): pl.pallas_call(functools.partial(kernel, shards, stages), out_shape=[jax....]
where the time goes in v8:
time: 46.6 us; the launch traced here: 46.4 us
  Pallas kernels  45.8 us (98%)
  between operations  0.64 us (1%)
    pallas_call x1, Pallas kernels, body(): pl.pallas_call(functools.partial(kernel, shards, stages), out_shape=[jax....  43.7 us
    pallas_call x1, Pallas kernels, body(): pl.pallas_call(write_out, out_shape=[jax.ShapeDtypeStruct(x.shape, x.dtyp...  2.11 us

profile of v8, /device:TPU:1, one launch (start us, length us, event | category | flops | bytes accessed | tf_op | source)
XLA Modules:
  0.0 46.4 jit_solution(2505529168805386654)
XLA Ops:
  0.6 43.7 %shard_map.127 = (bf16[128,512]{1,0:T(8,128)(2,1)}, bf16[128,512]{1,0:T(8,128)(2,1)}, bf16[128,512]{1,0:T(8,128)(2,1)}, bf16[128,512]{1,0:T(8,128)(2,1)}, f32[128,512]{1,0:T(8,128)}, /*index=5*/f32[128,512]{1,0:T(8,128)}) custom-call(bf16[128,512]{1,0:T(8,128)(2,1)} %bitcast.10, bf16[128,512]{1,0:T(8,128)(2,1)} %bitcast.11, bf16[128,512]{1,0:T(8,128)(2,1)} %bitcast.12, ...), custom_call_target="tpu_custom_call" | custom-call | tf_op jit(solution)/shard_map/pallas_call | solution.py:496
  44.3 2.1 %shard_map.128 = (bf16[128,512]{1,0:T(8,128)(2,1)}, bf16[128,512]{1,0:T(8,128)(2,1)}, bf16[128,512]{1,0:T(8,128)(2,1)}, bf16[128,512]{1,0:T(8,128)(2,1)}, f32[128,512]{1,0:T(8,128)}, /*index=5*/f32[128,512]{1,0:T(8,128)}) custom-call(bf16[128,512]{1,0:T(8,128)(2,1)} %get-tuple-element.18.refs_0_, bf16[128,512]{1,0:T(8,128)(2,1)} %get-tuple-element.19.refs_1_, ...), custom_call_target="tpu_custom_call" | custom-call | tf_op jit(solution)/shard_map/pallas_call | solution.py:526
